TPU v7x, 32 devices: a whole 2x2x4 slice. The times are simulated.
32 devices in a mesh: expert: 4 (over y, core), hidden: 8 (over z, x).
Axes of the slice: x: 2, y: 2, z: 4, core: 2. Of those that a mesh axis runs over, the one named last changes fastest.
Arguments:
- tokens: bfloat16 [16384, 512], P(('expert', 'hidden')), may hold values from -6 to 6
- lengths: int32 [32, 32], P(('expert', 'hidden')), may hold values from 1 to 128, 512 in all within a row
- task_ids: int32 [32, 32], P(('expert', 'hidden')), may hold values from 0 to 29
- expert_table: int32 [30, 2], replicated, may hold values from 0 to 7, all different within a row
- norm_gain: float32 [512, 3], P('hidden'), may hold values from 0.25 to 1.75
- norm_bias: float32 [512, 3], P('hidden'), may hold values from -1.5 to 1.5
- w_qkv: float32 [512, 1536], P('hidden', 'expert'), may hold values from -0.25 to 0.25
- w_out: float32 [512, 512], P('hidden', 'expert'), may hold values from -0.75 to 0.75
- w_in: float32 [512, 2048], P('hidden', 'expert'), may hold values from -0.25 to 0.25
- w_down: float32 [2048, 512], P('hidden', 'expert'), may hold values from -0.1875 to 0.1875
- w_router: float32 [512, 8], P('hidden', 'expert'), may hold values from -0.1875 to 0.1875
- expert_up: float32 [8, 512, 2048], P('expert', None, 'hidden'), may hold values from -0.25 to 0.25
- expert_down: float32 [8, 2048, 512], P('expert', 'hidden'), may hold values from -0.1875 to 0.1875
- cotangent: bfloat16 [16384, 512], P(('expert', 'hidden')), may hold values from -6 to 6
Outputs:
- layer_out: bfloat16 [16384, 512], P(('expert', 'hidden'))
- grad_tokens: float32 [16384, 512], P(('expert', 'hidden'))
- grad_gain: float32 [512, 3], P('hidden')
- grad_bias: float32 [512, 3], P('hidden')
- grad_qkv: float32 [512, 1536], P('hidden', 'expert')
- grad_out: float32 [512, 512], P('hidden', 'expert')
- grad_in: float32 [512, 2048], P('hidden', 'expert')
- grad_down: float32 [2048, 512], P('hidden', 'expert')
- grad_router: float32 [512, 8], P('hidden', 'expert')
- grad_expert_up: float32 [8, 512, 2048], P('expert', None, 'hidden')
- grad_expert_down: float32 [8, 2048, 512], P('expert', 'hidden')
Inputs may be any that keep to these rules, and one draw needn't show every extreme that they name: Each row holds the sentence lengths of one pack in order; they sum to 512, and the largest of every row is 128. `task_ids`: some tasks are much more frequent than others. `expert_table`: each row names two different experts; every expert is named by some task.
All inputs are finite; a program needn't handle non-finite values.
Results may differ from a plain program's by a relative error of at most 0.014.
The roundings to bfloat16 on the way count: a program that leaves them out, or rounds other values in their place, can miss the bound.
Values may be sent and summed in bfloat16 or wider, within the bound.
No kernel may reach another device: no remote copies, remote signals or barrier semaphores. Data moves between devices by JAX's collectives and lax.ppermute only.
A program may use at most 256 MiB of HBM per device.

v0:
```python
import math

import jax
import jax.numpy as jnp
from jax import lax
from jax.sharding import PartitionSpec as P

HEADS = 8
HEAD_DIM = 64


EPSILON = 1e-05
FILL_SCORE = -1000000000.0


def layer_norm(values, gain_vec, bias_vec):
    center = values - jnp.mean(values, axis=-1, keepdims=True)
    spread = jnp.mean(center * center, axis=-1, keepdims=True)
    return center * lax.rsqrt(spread + EPSILON) * gain_vec + bias_vec


def norm_back(values, gain_vec, bias_vec, incoming):
    _, pullback = jax.vjp(layer_norm, values, gain_vec, bias_vec)
    return pullback(incoming)


def gelu_tanh(values):
    return jax.nn.gelu(values, approximate=True)


def gelu_back(values, incoming):
    _, pullback = jax.vjp(gelu_tanh, values)
    return pullback(incoming)[0]


def token_routes(length_row, task_row, route_table, tok_count):
    sent_ends = jnp.cumsum(length_row)
    tok_index = jnp.arange(tok_count, dtype=jnp.int32)
    segment = jnp.sum((tok_index[:, None] >= sent_ends[None, :]).astype(jnp.int32), axis=1)
    sent_hot = (
        segment[:, None] == jnp.arange(length_row.shape[0], dtype=jnp.int32)[None, :]
    ).astype(jnp.int32)
    task_tok = jnp.sum(sent_hot * task_row[None, :], axis=1)
    task_hot = (
        task_tok[:, None] == jnp.arange(route_table.shape[0], dtype=jnp.int32)[None, :]
    ).astype(jnp.int32)
    pair_ids = jnp.sum(task_hot[:, :, None] * route_table[None, :, :], axis=1)
    return (segment, pair_ids)


def place_rows(pair_ids, expert_count, capacity):
    tok_count = pair_ids.shape[0]
    flat_ids = jnp.concatenate([pair_ids[:, 0], pair_ids[:, 1]])
    expert_hot = (flat_ids[:, None] == jnp.arange(expert_count, dtype=jnp.int32)[None, :]).astype(
        jnp.int32
    )
    earlier = jnp.cumsum(expert_hot, axis=0) - expert_hot
    row_rank = jnp.sum(earlier * expert_hot, axis=1)
    slot_of_row = jnp.where(
        row_rank < capacity, flat_ids * capacity + row_rank, expert_count * capacity
    )
    filler = jnp.full((expert_count * capacity + 1,), 2 * tok_count, jnp.int32)
    slot_row = filler.at[slot_of_row].set(jnp.arange(2 * tok_count, dtype=jnp.int32))
    return (slot_of_row, slot_row[: expert_count * capacity])


def local(
    tokens,
    lengths,
    task_ids,
    expert_table,
    norm_gain,
    norm_bias,
    w_qkv,
    w_out,
    w_in,
    w_down,
    w_router,
    expert_up,
    expert_down,
    cotangent,
):
    tok_count = tokens.shape[0]
    feat_dim = tokens.shape[1]
    local_experts = expert_up.shape[0]
    expert_count = lax.axis_size("expert") * local_experts
    capacity = 2 * tok_count // expert_count
    score_scale = 1.0 / math.sqrt(HEAD_DIM)
    col_gathered = (
        lax.all_gather(w_qkv.astype(jnp.bfloat16), "expert", axis=1, tiled=True),
        lax.all_gather(w_out.astype(jnp.bfloat16), "expert", axis=1, tiled=True),
        lax.all_gather(w_in.astype(jnp.bfloat16), "expert", axis=1, tiled=True),
        lax.all_gather(w_down.astype(jnp.bfloat16), "expert", axis=1, tiled=True),
        lax.all_gather(w_router.astype(jnp.bfloat16), "expert", axis=1, tiled=True),
    )
    qkv_mat, out_mat, in_mat, down_mat, route_mat, gain_low, bias_low = (
        lax.all_gather(col_gathered[0], "hidden", axis=0, tiled=True),
        lax.all_gather(col_gathered[1], "hidden", axis=0, tiled=True),
        lax.all_gather(col_gathered[2], "hidden", axis=0, tiled=True),
        lax.all_gather(col_gathered[3], "hidden", axis=0, tiled=True),
        lax.all_gather(col_gathered[4], "hidden", axis=0, tiled=True),
        lax.all_gather(norm_gain.astype(jnp.bfloat16), "hidden", axis=0, tiled=True),
        lax.all_gather(norm_bias.astype(jnp.bfloat16), "hidden", axis=0, tiled=True),
    )
    gain_all = gain_low.astype(jnp.float32)
    bias_all = bias_low.astype(jnp.float32)
    inputs = tokens.astype(jnp.float32)
    segment, pair_ids = token_routes(lengths[0], task_ids[0], expert_table, tok_count)
    normed_one = layer_norm(inputs, gain_all[:, 0], bias_all[:, 0]).astype(jnp.bfloat16)
    qkv_rows = jnp.dot(normed_one, qkv_mat, preferred_element_type=jnp.float32).astype(jnp.bfloat16)
    queries = qkv_rows[:, :feat_dim].reshape(tok_count, HEADS, HEAD_DIM)
    key_rows = qkv_rows[:, feat_dim : 2 * feat_dim].reshape(tok_count, HEADS, HEAD_DIM)
    values = qkv_rows[:, 2 * feat_dim :].reshape(tok_count, HEADS, HEAD_DIM)
    block_rows = min(512, tok_count)
    block_starts = jnp.arange(tok_count // block_rows, dtype=jnp.int32) * block_rows

    def block_scores():
        scores = (
            jnp.einsum("qhd,khd->hqk", queries, key_rows, preferred_element_type=jnp.float32)
            * score_scale
        )
        same_sent = segment[:, None] == segment[None, :]
        return (queries, jnp.where(same_sent[None], scores, FILL_SCORE))

    def attend(offset):
        _, scores = block_scores()
        row_peak = jnp.max(scores, axis=-1, keepdims=True)
        exp_scores = jnp.exp(scores - row_peak)
        row_total = jnp.sum(exp_scores, axis=-1, keepdims=True)
        prob_rows = exp_scores / row_total
        out_part = jnp.einsum(
            "hqk,khd->qhd",
            prob_rows.astype(jnp.bfloat16),
            values,
            preferred_element_type=jnp.float32,
        ).astype(jnp.bfloat16)
        return (out_part, row_peak[..., 0] + jnp.log(row_total[..., 0]))

    attended, log_totals = lax.map(attend, block_starts)
    attended = attended.reshape(tok_count, feat_dim)
    after_attn = inputs + jnp.dot(attended, out_mat, preferred_element_type=jnp.float32)
    normed_two = layer_norm(after_attn, gain_all[:, 1], bias_all[:, 1]).astype(jnp.bfloat16)
    pre_dense = jnp.dot(normed_two, in_mat, preferred_element_type=jnp.float32)
    hidden = gelu_tanh(pre_dense).astype(jnp.bfloat16)
    layer_two = after_attn + jnp.dot(hidden, down_mat, preferred_element_type=jnp.float32)
    normed_three = layer_norm(layer_two, gain_all[:, 2], bias_all[:, 2]).astype(jnp.bfloat16)
    logits = jnp.dot(normed_three, route_mat, preferred_element_type=jnp.float32)
    pick_hot = pair_ids[:, :, None] == jnp.arange(expert_count, dtype=jnp.int32)[None, None, :]
    chosen = jnp.sum(jnp.where(pick_hot, logits[:, None, :], 0.0), axis=2)
    gate_vals = jax.nn.softmax(chosen, axis=-1)
    slot_of_row, slot_row = place_rows(pair_ids, expert_count, capacity)
    row_token = jnp.where(slot_row < 2 * tok_count, slot_row % tok_count, tok_count)
    padded = jnp.concatenate([normed_three, jnp.zeros((1, feat_dim), jnp.bfloat16)])
    sent_rows = padded[row_token].reshape(-1, local_experts, capacity, feat_dim)
    received = lax.all_to_all(sent_rows, "expert", split_axis=0, concat_axis=0, tiled=True)
    up_local = expert_up.astype(jnp.bfloat16)
    down_local = expert_down.astype(jnp.bfloat16)
    pieces = lax.all_gather(received, "hidden", axis=0, tiled=True)
    pre_part = jnp.einsum("secd,edf->secf", pieces, up_local, preferred_element_type=jnp.float32)
    group_rows = pieces
    expert_pre = pre_part
    expert_hidden = gelu_tanh(pre_part).astype(jnp.bfloat16)
    expert_result = lax.psum_scatter(
        jnp.einsum("secf,efd->secd", expert_hidden, down_local, preferred_element_type=jnp.float32),
        "hidden",
        scatter_dimension=0,
        tiled=True,
    ).astype(jnp.bfloat16)
    returned = lax.all_to_all(expert_result, "expert", split_axis=0, concat_axis=0, tiled=True)
    returned = jnp.concatenate(
        [
            returned.reshape(expert_count * capacity, feat_dim),
            jnp.zeros((1, feat_dim), jnp.bfloat16),
        ]
    )
    picked = returned[slot_of_row].astype(jnp.float32).reshape(2, tok_count, feat_dim)
    layer_out = layer_two + gate_vals[:, 0:1] * picked[0] + gate_vals[:, 1:2] * picked[1]
    upstream = cotangent.astype(jnp.float32)
    gate_grad = jnp.stack(
        [jnp.sum(upstream * picked[0], axis=1), jnp.sum(upstream * picked[1], axis=1)], axis=1
    )
    chosen_grad = gate_vals * (gate_grad - jnp.sum(gate_vals * gate_grad, axis=1, keepdims=True))
    logit_grad = jnp.sum(jnp.where(pick_hot, chosen_grad[:, :, None], 0.0), axis=1).astype(
        jnp.bfloat16
    )
    row_grads = jnp.concatenate(
        [gate_vals[:, 0:1] * upstream, gate_vals[:, 1:2] * upstream]
    ).astype(jnp.bfloat16)
    row_grads = jnp.concatenate([row_grads, jnp.zeros((1, feat_dim), jnp.bfloat16)])
    grad_sent = row_grads[slot_row].reshape(-1, local_experts, capacity, feat_dim)
    grad_received = lax.all_to_all(grad_sent, "expert", split_axis=0, concat_axis=0, tiled=True)
    pieces = lax.all_gather(grad_received, "hidden", axis=0, tiled=True)
    pre_part = expert_pre
    hidden_grad = jnp.einsum(
        "secd,efd->secf", pieces, down_local, preferred_element_type=jnp.float32
    )
    pre_grads = gelu_back(pre_part, hidden_grad).astype(jnp.bfloat16)
    grad_expert_down = jnp.einsum(
        "secf,secd->efd", expert_hidden, pieces, preferred_element_type=jnp.float32
    )
    grad_expert_up = jnp.einsum(
        "secd,secf->edf", group_rows, pre_grads, preferred_element_type=jnp.float32
    )
    input_grads = lax.psum_scatter(
        jnp.einsum("secf,edf->secd", pre_grads, up_local, preferred_element_type=jnp.float32),
        "hidden",
        scatter_dimension=0,
        tiled=True,
    ).astype(jnp.bfloat16)
    back_grads = lax.all_to_all(input_grads, "expert", split_axis=0, concat_axis=0, tiled=True)
    back_grads = jnp.concatenate(
        [
            back_grads.reshape(expert_count * capacity, feat_dim),
            jnp.zeros((1, feat_dim), jnp.bfloat16),
        ]
    )
    token_grads = back_grads[slot_of_row].astype(jnp.float32).reshape(2, tok_count, feat_dim)
    three_grad = (
        token_grads[0]
        + token_grads[1]
        + jnp.dot(logit_grad, route_mat.T, preferred_element_type=jnp.float32)
    )
    grad_router = jnp.dot(normed_three.T, logit_grad, preferred_element_type=jnp.float32)
    two_part, gain_three, bias_three = norm_back(
        layer_two, gain_all[:, 2], bias_all[:, 2], three_grad
    )
    two_grad_in = upstream + two_part
    ffn_grad = two_grad_in.astype(jnp.bfloat16)
    grad_down = jnp.dot(hidden.T, ffn_grad, preferred_element_type=jnp.float32)
    dense_pre_grad = gelu_back(
        pre_dense, jnp.dot(ffn_grad, down_mat.T, preferred_element_type=jnp.float32)
    ).astype(jnp.bfloat16)
    grad_in = jnp.dot(normed_two.T, dense_pre_grad, preferred_element_type=jnp.float32)
    normed_two_grad = jnp.dot(dense_pre_grad, in_mat.T, preferred_element_type=jnp.float32)
    after_part, gain_two, bias_two = norm_back(
        after_attn, gain_all[:, 1], bias_all[:, 1], normed_two_grad
    )
    after_grad = two_grad_in + after_part
    attn_grad = after_grad.astype(jnp.bfloat16)
    grad_out = jnp.dot(attended.T, attn_grad, preferred_element_type=jnp.float32)
    attended_grad = (
        jnp.dot(attn_grad, out_mat.T, preferred_element_type=jnp.float32)
        .astype(jnp.bfloat16)
        .reshape(tok_count, HEADS, HEAD_DIM)
    )

    def attend_back(carried, element):
        key_grad, value_grad = carried
        offset, log_total = element
        query_part, scores = block_scores()
        prob_rows = jnp.exp(scores - log_total[..., None])
        prob_grad = jnp.einsum(
            "qhd,khd->hqk", attended_grad, values, preferred_element_type=jnp.float32
        )
        value_grad = value_grad + jnp.einsum(
            "hqk,qhd->khd",
            prob_rows.astype(jnp.bfloat16),
            attended_grad,
            preferred_element_type=jnp.float32,
        )
        score_grad = (
            prob_rows * (prob_grad - jnp.sum(prob_grad * prob_rows, axis=-1, keepdims=True))
        ).astype(jnp.bfloat16)
        query_grad = (
            jnp.einsum("hqk,khd->qhd", score_grad, key_rows, preferred_element_type=jnp.float32)
            * score_scale
        )
        key_grad = (
            key_grad
            + jnp.einsum("hqk,qhd->khd", score_grad, query_part, preferred_element_type=jnp.float32)
            * score_scale
        )
        return ((key_grad, value_grad), query_grad)

    zero_grads = jnp.zeros((tok_count, HEADS, HEAD_DIM), jnp.float32)
    (key_grad, value_grad), query_grad = lax.scan(
        attend_back, (zero_grads, zero_grads), (block_starts, log_totals)
    )
    qkv_grad = jnp.concatenate(
        [
            query_grad.reshape(tok_count, feat_dim),
            key_grad.reshape(tok_count, feat_dim),
            value_grad.reshape(tok_count, feat_dim),
        ],
        axis=1,
    ).astype(jnp.bfloat16)
    grad_qkv = jnp.dot(normed_one.T, qkv_grad, preferred_element_type=jnp.float32)
    normed_one_grad = jnp.dot(qkv_grad, qkv_mat.T, preferred_element_type=jnp.float32)
    input_part, gain_one, bias_one = norm_back(
        inputs, gain_all[:, 0], bias_all[:, 0], normed_one_grad
    )
    grad_tokens = after_grad + input_part
    gain_grad = jnp.stack([gain_one, gain_two, gain_three], axis=1)
    bias_grad = jnp.stack([bias_one, bias_two, bias_three], axis=1)
    summed = (
        lax.psum_scatter(grad_qkv, "hidden", scatter_dimension=0, tiled=True),
        lax.psum_scatter(grad_out, "hidden", scatter_dimension=0, tiled=True),
        lax.psum_scatter(grad_in, "hidden", scatter_dimension=0, tiled=True),
        lax.psum_scatter(grad_down, "hidden", scatter_dimension=0, tiled=True),
        lax.psum_scatter(grad_router, "hidden", scatter_dimension=0, tiled=True),
        lax.psum_scatter(gain_grad, "hidden", scatter_dimension=0, tiled=True),
        lax.psum_scatter(bias_grad, "hidden", scatter_dimension=0, tiled=True),
    )
    reduced = (
        lax.psum_scatter(summed[0], "expert", scatter_dimension=1, tiled=True),
        lax.psum_scatter(summed[1], "expert", scatter_dimension=1, tiled=True),
        lax.psum_scatter(summed[2], "expert", scatter_dimension=1, tiled=True),
        lax.psum_scatter(summed[3], "expert", scatter_dimension=1, tiled=True),
        lax.psum_scatter(summed[4], "expert", scatter_dimension=1, tiled=True),
    )
    gain_total, bias_total = lax.psum((summed[5], summed[6]), "expert")
    return (
        layer_out.astype(jnp.bfloat16),
        grad_tokens,
        gain_total,
        bias_total,
        reduced[0],
        reduced[1],
        reduced[2],
        reduced[3],
        reduced[4],
        grad_expert_up,
        grad_expert_down,
    )


def solution(mesh):
    return jax.shard_map(
        local,
        mesh=mesh,
        in_specs=(
            P(("expert", "hidden"), None),
            P(("expert", "hidden"), None),
            P(("expert", "hidden"), None),
            P(),
            P("hidden", None),
            P("hidden", None),
            P("hidden", "expert"),
            P("hidden", "expert"),
            P("hidden", "expert"),
            P("hidden", "expert"),
            P("hidden", "expert"),
            P("expert", None, "hidden"),
            P("expert", "hidden", None),
            P(("expert", "hidden"), None),
        ),
        out_specs=(
            P(("expert", "hidden"), None),
            P(("expert", "hidden"), None),
            P("hidden", None),
            P("hidden", None),
            P("hidden", "expert"),
            P("hidden", "expert"),
            P("hidden", "expert"),
            P("hidden", "expert"),
            P("hidden", "expert"),
            P("expert", None, "hidden"),
            P("expert", "hidden", None),
        ),
        check_vma=False,
    )
```

profile of v0, /device:TPU:0, one launch (start us, length us, event | category | flops | bytes accessed | tf_op | source)
XLA Modules:
  0.0 2428.3 jit_solution(18322122461316016161)
XLA Ops:
  8.2 7.3 all_gather.44
  16.5 6.4 all_gather.48
  23.9 6.3 all_gather.50
  34.3 20.9 all-gather.1
  55.3 16.3 all-gather
  87.8 32.9 %all_gather.47 = bf16[512,512]{1,0:T(8,128)(2,1)S(1)} all-gather(bf16[64,512]{1,0:T(8,128)(2,1)S(1)} %all_gather.46), channel_id=1, replica_groups=mesh['expert'=4,'hidden'=8] {'hidden'}, dimensions={0}, use_global_device_ids=true | all-gather | bytes 589824 | tf_op jit(solution)/shard_map/all_gather | solution.py:98
  136.3 33.4 %all-gather.14.cloned.1.call-done = bf16[2048,512]{1,0:T(8,128)(2,1)} async-done(((bf16[256,512]{1,0:T(8,128)(2,1)}), bf16[2048,512]{1,0:T(8,128)(2,1)}) %all-gather.14.cloned.1.call-update) | async-done | bytes 2097168 | tf_op jit(solution)/shard_map/all_gather | solution.py:100
  179.4 17.1 all_to_all.20
  202.8 26.5 %all-gather.3 = bf16[8,64,8]{1,2,0:T(8,128)(2,1)S(1)} all-gather(bf16[1,64,8]{1,2,0:T(8,128)(2,1)S(1)} %bitcast.243), channel_id=1, replica_groups=mesh['expert'=4,'hidden'=8] {'hidden'}, dimensions={0}, use_global_device_ids=true | all-gather | bytes 9216 | tf_op jit(solution)/shard_map/all_gather | solution.py:101
  234.0 17.5 all_to_all.21
  254.0 66.6 %all-gather.16.cloned.1.call-done = bf16[32,2,128,512]{3,2,0,1:T(8,128)(2,1)} async-done(((bf16[4,2,128,512]{3,2,0,1:T(8,128)(2,1)}), bf16[32,2,128,512]{3,2,0,1:T(8,128)(2,1)}) %all-gather.16.cloned.1.call-update) | async-done | bytes 8388624 | tf_op jit(solution)/shard_map/all_gather | solution.py:158
  330.0 7.2 convolution_bitcast_fusion.1
  337.2 109.1 %all-gather.18.cloned.1.call-done = bf16[32,2,128,512]{3,2,0,1:T(8,128)(2,1)} async-done(((bf16[4,2,128,512]{3,2,0,1:T(8,128)(2,1)}), bf16[32,2,128,512]{3,2,0,1:T(8,128)(2,1)}) %all-gather.18.cloned.1.call-update) | async-done | bytes 8388624 | tf_op jit(solution)/shard_map/all_gather | solution.py:192
  446.3 13.1 fusion.6
  461.3 8.1 convolution_bitcast_fusion
  469.4 1278.8 %all-reduce.10 = (bf16[32,2,128,512]{3,2,0,1:T(8,128)(2,1)}, bf16[32,2,128,512]{3,2,0,1:T(8,128)(2,1)}) all-reduce(f32[32,2,128,512]{3,2,0,1:T(8,128)} %convolution_bitcast_fusion.1, f32[32,2,128,512]{3,2,0,1:T(8,128)} %convolution_bitcast_fusion), channel_id=2, replica_groups=mesh['expert'=4,'hidden'=8] {'hidden'}, use_global_device_ids=true, to_apply=%region_19.20.clone | all-reduce | flops 8388608 | bytes 50331648
  1756.6 12.0 all-to-all-done.1
  1773.2 14.2 all-to-all-done.3
  1847.3 27.3 %reduce-scatter.28.cloned.1.call-done = f32[64,512]{1,0:T(8,128)} async-done(((f32[512,512]{1,0:T(8,128)}), f32[64,512]{1,0:T(8,128)}) %reduce-scatter.28.cloned.1.call-update) | async-done | bytes 131088 | tf_op jit(solution)/shard_map/reduce_scatter | solution.py:297
  1874.6 77.3 %reduce-scatter.24.cloned.1.call-done = f32[64,1536]{1,0:T(8,128)} async-done(((f32[512,1536]{1,0:T(8,128)}), f32[64,1536]{1,0:T(8,128)}) %reduce-scatter.24.cloned.1.call-update) | async-done | bytes 393232 | tf_op jit(solution)/shard_map/reduce_scatter | solution.py:296
  1953.2 89.8 %reduce-scatter.36.cloned.1.call-done = f32[256,512]{1,0:T(8,128)} async-done(((f32[2048,512]{1,0:T(8,128)}), f32[256,512]{1,0:T(8,128)}) %reduce-scatter.36.cloned.1.call-update) | async-done | bytes 524304 | tf_op jit(solution)/shard_map/reduce_scatter | solution.py:299
  2043.3 9.8 convolution_bitcast_fusion.2
  2053.1 81.2 %reduce-scatter.32.cloned.1.call-done = f32[64,2048]{1,0:T(8,128)} async-done(((f32[512,2048]{1,0:T(8,128)}), f32[64,2048]{1,0:T(8,128)}) %reduce-scatter.32.cloned.1.call-update) | async-done | bytes 524304 | tf_op jit(solution)/shard_map/reduce_scatter | solution.py:298
  2134.3 8.9 convolution_bitcast_fusion.3
  2144.6 54.3 %reduce-scatter.40.cloned.1.call-done = f32[64,3]{1,0:T(8,128)} async-done(((f32[512,3]{1,0:T(8,128)}), f32[64,3]{1,0:T(8,128)}) %reduce-scatter.40.cloned.1.call-update) | async-done | bytes 784
  2199.7 63.1 %reduce-scatter.42.cloned.1.call-done = f32[64,3]{1,0:T(8,128)} async-done(((f32[512,3]{1,0:T(8,128)}), f32[64,3]{1,0:T(8,128)}) %reduce-scatter.42.cloned.1.call-update) | async-done | bytes 784
  2263.6 63.0 %reduce-scatter.44.cloned.1.call-done = f32[64,8]{1,0:T(8,128)} async-done(((f32[512,8]{1,0:T(8,128)}), f32[64,8]{1,0:T(8,128)}) %reduce-scatter.44.cloned.1.call-update) | async-done | bytes 2064
  2327.4 6.3 all-reduce.8
  2334.3 14.1 reduce-scatter.30.cloned.1.call-done
  2348.4 23.8 reduce-scatter.26.cloned.1.call-done
  2372.1 24.6 %reduce-scatter.38.cloned.1.call-done = f32[256,128]{1,0:T(8,128)} async-done(((f32[256,512]{1,0:T(8,128)}), f32[256,128]{1,0:T(8,128)}) %reduce-scatter.38.cloned.1.call-update) | async-done | bytes 131088 | tf_op jit(solution)/shard_map/reduce_scatter | solution.py:308
  2396.7 24.8 %reduce-scatter.34.cloned.1.call-done = f32[64,512]{1,0:T(8,128)} async-done(((f32[64,2048]{1,0:T(8,128)}), f32[64,512]{1,0:T(8,128)}) %reduce-scatter.34.cloned.1.call-update) | async-done | bytes 131088 | tf_op jit(solution)/shard_map/reduce_scatter | solution.py:307
  (245 shorter events, 149.9 us)
Async XLA Ops:
  7.2 113.5 %copy-start.4 = (bf16[512,512]{1,0:T(8,128)(2,1)S(1)}, bf16[512,512]{1,0:T(8,128)(2,1)}, u32[]{:S(2)}) copy-start(bf16[512,512]{1,0:T(8,128)(2,1)} %param.14) | copy-start | bytes 1572868
  7.2 113.5 %all-gather.10.cloned.1.call-start = ((), (), s32[]{:S(2)}) async-start(), calls=%async_computation.15 | async-start | bytes 1769472 | tf_op jit(solution)/shard_map/all_gather | solution.py:97
  15.5 115.9 %all-gather.12.cloned.1.call-start = ((), (), s32[]{:S(2)}) async-start(), calls=%async_computation.16 | async-start | bytes 2359296 | tf_op jit(solution)/shard_map/all_gather | solution.py:99
  23.0 146.8 %all-gather.14.cloned.1.call-start = ((), (), s32[]{:S(2)}) async-start(), calls=%async_computation.17 | async-start | bytes 2359296 | tf_op jit(solution)/shard_map/all_gather | solution.py:100
  30.3 290.3 %all-gather.16.cloned.1.call-start = ((), (), s32[]{:S(2)}) async-start(), calls=%async_computation.18 | async-start | bytes 9437184 | tf_op jit(solution)/shard_map/all_gather | solution.py:158
  120.7 9.9 copy-start.16
  130.6 5.7 copy-start.24
  175.4 54.0 %copy-start.6 = (bf16[512,512]{1,0:T(8,128)(2,1)}, bf16[512,512]{1,0:T(8,128)(2,1)S(1)}, u32[]{:S(2)}) copy-start(bf16[512,512]{1,0:T(8,128)(2,1)S(1)} %add_convert_fusion.1) | copy-start | bytes 1572868
  179.4 18.3 copy-start.35
  179.4 50.3 %copy-start.8 = (bf16[512,512]{1,0:T(8,128)(2,1)S(1)}, bf16[512,512]{1,0:T(8,128)(2,1)}, u32[]{:S(2)}) copy-start(bf16[512,512]{1,0:T(8,128)(2,1)} %param.27) | copy-start | bytes 1572868
  197.7 248.6 %all-gather.18.cloned.1.call-start = ((), (), s32[]{:S(2)}) async-start(), calls=%async_computation.19 | async-start | bytes 9437184 | tf_op jit(solution)/shard_map/all_gather | solution.py:192
  234.0 18.7 copy-start.37
  234.0 86.5 %copy-start.21 = (f32[2,512,256]{2,1,0:T(8,128)S(1)}, f32[2,512,256]{2,1,0:T(8,128)}, u32[]{:S(2)}) copy-start(f32[2,512,256]{2,1,0:T(8,128)} %param.25) | copy-start | bytes 3145732
  253.9 76.0 %copy-start.28 = (f32[2,256,512]{2,1,0:T(8,128)S(1)}, f32[2,256,512]{2,1,0:T(8,128)}, u32[]{:S(2)}) copy-start(f32[2,256,512]{2,1,0:T(8,128)} %param.26) | copy-start | bytes 3145732
  1750.6 18.0 all-to-all-start.1
  1768.6 18.8 all-to-all-start.3
  1772.8 101.7 %reduce-scatter.28.cloned.1.call-start = ((), (), s32[]{:S(2)}) async-start(), calls=%async_computation.22 | async-start | bytes 1179648 | tf_op jit(solution)/shard_map/reduce_scatter | solution.py:297
  1793.7 6.7 copy-start.18
  1811.7 7.2 copy-start.14
  1813.1 138.8 %reduce-scatter.24.cloned.1.call-start = ((), (), s32[]{:S(2)}) async-start(), calls=%async_computation.20 | async-start | bytes 3538944 | tf_op jit(solution)/shard_map/reduce_scatter | solution.py:296
  1813.4 5.9 slice-start.1
  1829.4 213.6 %reduce-scatter.36.cloned.1.call-start = ((), (), s32[]{:S(2)}) async-start(), calls=%async_computation.26 | async-start | bytes 4718592 | tf_op jit(solution)/shard_map/reduce_scatter | solution.py:299
  1835.5 298.8 %reduce-scatter.32.cloned.1.call-start = ((), (), s32[]{:S(2)}) async-start(), calls=%async_computation.24 | async-start | bytes 4718592 | tf_op jit(solution)/shard_map/reduce_scatter | solution.py:298
  1840.5 5.7 copy-start.7
  1840.5 358.4 %reduce-scatter.40.cloned.1.call-start = ((), (), s32[]{:S(2)}) async-start(), calls=%async_computation.28 | async-start | bytes 294912
  1843.7 108.3 %copy-start.36 = (u32[32]{0:T(128)S(1)}, u32[32]{0:T(128)}, u32[]{:S(2)}) copy-start(u32[32]{0:T(128)} %constant.138) | copy-start | bytes 388
  1845.2 417.6 %reduce-scatter.42.cloned.1.call-start = ((), (), s32[]{:S(2)}) async-start(), calls=%async_computation.29 | async-start | bytes 294912
  1846.1 480.5 %reduce-scatter.44.cloned.1.call-start = ((), (), s32[]{:S(2)}) async-start(), calls=%async_computation.30 | async-start | bytes 294912
  1847.3 501.1 %reduce-scatter.30.cloned.1.call-start = ((), (), s32[]{:S(2)}) async-start(), calls=%async_computation.23 | async-start | bytes 163840 | tf_op jit(solution)/shard_map/reduce_scatter | solution.py:306
  1874.6 497.5 %reduce-scatter.26.cloned.1.call-start = ((), (), s32[]{:S(2)}) async-start(), calls=%async_computation.21 | async-start | bytes 491520 | tf_op jit(solution)/shard_map/reduce_scatter | solution.py:305
  1951.9 444.8 %reduce-scatter.38.cloned.1.call-start = ((), (), s32[]{:S(2)}) async-start(), calls=%async_computation.27 | async-start | bytes 655360 | tf_op jit(solution)/shard_map/reduce_scatter | solution.py:308
  2043.0 378.5 %reduce-scatter.34.cloned.1.call-start = ((), (), s32[]{:S(2)}) async-start(), calls=%async_computation.25 | async-start | bytes 655360 | tf_op jit(solution)/shard_map/reduce_scatter | solution.py:307
  (26 other events, 60.1 us)
Sparse Core Ops, SparseCore 0:
  15.7 45.7 all-gather.9
  63.5 54.7 all-gather.11
  120.5 49.1 all-gather.13
  197.8 122.7 all-gather.15
  323.2 123.0 all-gather.17
  1813.2 61.2 reduce-scatter.27
  1878.6 73.2 reduce-scatter.23
  1955.9 86.9 reduce-scatter.35
  2046.6 87.6 reduce-scatter.31
  2137.8 60.9 reduce-scatter.39
  2202.5 60.2 reduce-scatter.41
  2266.3 60.2 reduce-scatter.43
  2329.7 18.5 reduce-scatter.29
  2351.3 20.7 reduce-scatter.25
  2375.0 21.6 reduce-scatter.37
  2399.8 21.6 reduce-scatter.33
where the time goes:
time: 2430 us
  blocking collectives  1450 us (60%)
  waiting for transfers between devices  779 us (32%)
  matrix products  104 us (4%)
  local copies, waits for them, and re-layouts  50.9 us (2%)
    unnamed x1, blocking collectives  1280 us
    unnamed x19, waiting for transfers between devices  181 us
    all_gather x1, waiting for transfers between devices, local(): pieces = lax.all_gather(grad_received, 'hidden', axis=0, tiled=True)  109 us
    reduce_scatter x1, waiting for transfers between devices, local(): lax.psum_scatter(grad_down, 'hidden', scatter_dimension=0, tiled=True)  89.8 us
    reduce_scatter x1, waiting for transfers between devices, local(): lax.psum_scatter(grad_in, 'hidden', scatter_dimension=0, tiled=True)  81.2 us
    reduce_scatter x1, waiting for transfers between devices, local(): lax.psum_scatter(grad_qkv, 'hidden', scatter_dimension=0, tiled=True)  77.3 us
    all_gather x1, waiting for transfers between devices, local(): pieces = lax.all_gather(received, 'hidden', axis=0, tiled=True)  66.6 us
  transfers between devices with their start and end apart: 18, of which 16 were waited for; matrix products, arithmetic and copies ran while one was open for 4% of the time, Pallas kernels for 0%

commit v1 on v0

v1 whole, which is shorter than its diff:
```python
import functools
import math

import jax
import jax.numpy as jnp
from jax import lax
from jax.experimental import pallas as pl
from jax.experimental.pallas import tpu as pltpu
from jax.sharding import Mesh, PartitionSpec as P

HEAD_DIM = 64
MAXLEN = 128
LANES = 128
EPSILON = 1e-05
FILL_SCORE = -1000000000.0
AXES = ("y", "c", "z", "x")
VMEM_BYTES = 56 * 1024 * 1024
GELU_A = math.sqrt(2.0 / math.pi)
GELU_B = 0.044715

F32 = jnp.float32
BF16 = jnp.bfloat16

NN = (((1,), (0,)), ((), ()))
NT = (((1,), (1,)), ((), ()))
TN = (((0,), (0,)), ((), ()))


def mm(a, b, dims=NN):
    return lax.dot_general(a, b, dims, preferred_element_type=F32)


def gelu(v):
    t = jnp.tanh(GELU_A * (v + GELU_B * (v * v * v)))
    return 0.5 * v * (1.0 + t)


def gelu_both(v):
    v2 = v * v
    t = jnp.tanh(GELU_A * (v + GELU_B * (v2 * v)))
    half = 0.5 * (1.0 + t)
    slope = half + 0.5 * v * (1.0 - t * t) * (GELU_A + (3.0 * GELU_A * GELU_B) * v2)
    return v * half, slope


def norm_parts(v):
    center = v - jnp.mean(v, axis=-1, keepdims=True)
    r = lax.rsqrt(jnp.mean(center * center, axis=-1, keepdims=True) + EPSILON)
    return center * r, r


def norm_back(xhat, r, gain, h):
    hg = h * gain
    inner = jnp.mean(hg * xhat, axis=-1, keepdims=True)
    dv = r * (hg - jnp.mean(hg, axis=-1, keepdims=True) - xhat * inner)
    return dv, jnp.sum(h * xhat, axis=0, keepdims=True), jnp.sum(h, axis=0, keepdims=True)


def params(**kw):
    return pltpu.CompilerParams(vmem_limit_bytes=VMEM_BYTES, **kw)


def vmem():
    return pl.BlockSpec(memory_space=pltpu.VMEM)


def smem():
    return pl.BlockSpec(memory_space=pltpu.SMEM)


def anywhere():
    return pl.BlockSpec(memory_space=pl.ANY)


class Layout:
    def __init__(self, sizes):
        self.sizes = sizes
        self.count = math.prod(sizes.values())

    def owner(self, me_ref, k, order):
        at = {}
        for axis in reversed(order):
            n = self.sizes[axis]
            at[axis] = lax.bitwise_xor(me_ref[AXES.index(axis)], lax.rem(k, n))
            k = lax.div(k, n)
        return at["y"] * self.sizes["c"] + at["c"], at["z"] * self.sizes["x"] + at["x"]


def move_pieces(layout, me_ref, order, stack_ref, parts, sem, inward):
    @pl.loop(0, layout.count)
    def _(k):
        e, h = layout.owner(me_ref, k, order)
        for whole, rows, cols, first in parts:
            piece = stack_ref.at[k, :, pl.ds(first, cols)]
            block = whole.at[
                pl.ds(pl.multiple_of(h * rows, rows), rows),
                pl.ds(pl.multiple_of(e * cols, cols), cols),
            ]
            src, dst = (piece, block) if inward else (block, piece)
            pltpu.make_async_copy(src, dst, sem).start()


def wait_all(ref, sem):
    pltpu.make_async_copy(ref, ref, sem).wait()


def routes_kernel(capacity, experts, len_row, len_col, task_row, task_col, table, table_t, rows_out, cols_out):
    sents = len_row.shape[1]
    tasks = table.shape[0]
    toks = rows_out.shape[1]
    f = lambda v: v.astype(F32)
    i0 = lax.broadcasted_iota(jnp.int32, (sents, sents), 0)
    i1 = lax.broadcasted_iota(jnp.int32, (sents, sents), 1)
    ends_row = jnp.sum(jnp.where(i0 <= i1, f(len_col[...]), 0.0), axis=0, keepdims=True)
    ends_col = jnp.sum(jnp.where(i1 <= i0, f(len_row[...]), 0.0), axis=1, keepdims=True)
    starts_row = ends_row - f(len_row[...])
    starts_col = ends_col - f(len_col[...])
    tok = f(lax.broadcasted_iota(jnp.int32, (toks, sents), 0))
    sent = lax.broadcasted_iota(jnp.int32, (toks, sents), 1)
    hot = (tok >= starts_row) & (tok < ends_row)
    seg_c = jnp.sum(jnp.where(hot, f(sent), 0.0), axis=1, keepdims=True)
    task_c = jnp.sum(jnp.where(hot, f(task_row[...]), 0.0), axis=1, keepdims=True)
    thot = f(lax.broadcasted_iota(jnp.int32, (toks, tasks), 1)) == task_c
    pair_c = [
        jnp.sum(jnp.where(thot, f(table_t[c : c + 1, :]), 0.0), axis=1, keepdims=True)
        for c in range(2)
    ]
    tok = f(lax.broadcasted_iota(jnp.int32, (sents, toks), 1))
    sent = lax.broadcasted_iota(jnp.int32, (sents, toks), 0)
    hot = (tok >= starts_col) & (tok < ends_col)
    seg_r = jnp.sum(jnp.where(hot, f(sent), 0.0), axis=0, keepdims=True)
    task_r = jnp.sum(jnp.where(hot, f(task_col[...]), 0.0), axis=0, keepdims=True)
    thot = f(lax.broadcasted_iota(jnp.int32, (tasks, toks), 0)) == task_r
    pair_r = [
        jnp.sum(jnp.where(thot, f(table[:, c : c + 1]), 0.0), axis=0, keepdims=True)
        for c in range(2)
    ]
    a0 = lax.broadcasted_iota(jnp.int32, (toks, toks), 0)
    a1 = lax.broadcasted_iota(jnp.int32, (toks, toks), 1)
    upper = (a0 < a1).astype(BF16)
    lower = (a1 < a0).astype(BF16)
    er = f(lax.broadcasted_iota(jnp.int32, (experts, toks), 0))
    ec = f(lax.broadcasted_iota(jnp.int32, (toks, experts), 1))
    hot_r = [(er == pair_r[c]).astype(F32) for c in range(2)]
    hot_c = [(ec == pair_c[c]).astype(F32) for c in range(2)]
    before_r = [mm(hot_r[c].astype(BF16), upper) for c in range(2)]
    before_c = [mm(lower, hot_c[c].astype(BF16)) for c in range(2)]
    before_r[1] = before_r[1] + jnp.sum(hot_r[0], axis=1, keepdims=True)
    before_c[1] = before_c[1] + jnp.sum(hot_c[0], axis=0, keepdims=True)
    slot_r, slot_c = [], []
    for c in range(2):
        rank = jnp.sum(hot_r[c] * before_r[c], axis=0, keepdims=True)
        slot_r.append(jnp.where(rank < capacity, pair_r[c] * capacity + rank, -1.0))
        rank = jnp.sum(hot_c[c] * before_c[c], axis=1, keepdims=True)
        slot_c.append(jnp.where(rank < capacity, pair_c[c] * capacity + rank, -1.0))
    at = lax.broadcasted_iota(jnp.int32, rows_out.shape, 0)
    rows_out[...] = jnp.where(
        at == 0, seg_r, jnp.where(at == 1, slot_r[0], slot_r[1])
    ).astype(jnp.int32)
    at = lax.broadcasted_iota(jnp.int32, cols_out.shape, 1)
    packed = jnp.where(at == 0, seg_c, 0.0)
    for j, v in enumerate((pair_c[0], pair_c[1], slot_c[0], slot_c[1])):
        packed = jnp.where(at == j + 1, v, packed)
    cols_out[...] = packed.astype(jnp.int32)


def find_routes(lengths, task_ids, expert_table, toks, experts, capacity):
    return pl.pallas_call(
        functools.partial(routes_kernel, capacity, experts),
        out_shape=(
            jax.ShapeDtypeStruct((8, toks), jnp.int32),
            jax.ShapeDtypeStruct((toks, 8), jnp.int32),
        ),
        in_specs=[vmem()] * 6,
        out_specs=(vmem(), vmem()),
        compiler_params=params(),
        name="routes",
    )(lengths, lengths.T, task_ids, task_ids.T, expert_table, expert_table.T)


def head_blocks(toks):
    n = toks // MAXLEN
    return [(i * MAXLEN, max(i - 1, 0) * MAXLEN, min(i + 2, n) * MAXLEN) for i in range(n)]


def two_heads(block, low_half):
    zero = jnp.zeros_like(block)
    return jnp.concatenate([jnp.where(low_half, block, zero), jnp.where(low_half, zero, block)], axis=0)


def pick_heads(stacked, low_half):
    n = stacked.shape[0] // 2
    return jnp.where(low_half, stacked[:n], stacked[n:])


def probabilities(q2, keys, mask):
    scores = mm(q2, keys, NT) * (1.0 / math.sqrt(HEAD_DIM))
    scores = jnp.where(mask, scores, FILL_SCORE)
    exps = jnp.exp(scores - jnp.max(scores, axis=-1, keepdims=True))
    return exps * (1.0 / jnp.sum(exps, axis=-1, keepdims=True))


def same_sentence(cols_ref, rows_ref, q0, k0, k1):
    seg = cols_ref[q0 : q0 + MAXLEN, 0:1]
    return jnp.concatenate([seg, seg], axis=0) == rows_ref[0:1, k0:k1]


def load_qo(layout, me_ref, refs, qkv_w, out_w, sem):
    if len(refs) == 1:
        rows = refs[0].shape[1]
        share = layout.sizes["y"] * layout.sizes["c"]
        move_pieces(
            layout,
            me_ref,
            ("c", "y", "x", "z"),
            refs[0],
            [
                (qkv_w, rows, qkv_w.shape[1] // share, 0),
                (out_w, rows, out_w.shape[1] // share, qkv_w.shape[1] // share),
            ],
            sem,
            True,
        )
    else:
        pltpu.make_async_copy(refs[0], qkv_w, sem).start()
        pltpu.make_async_copy(refs[1], out_w, sem).start()


def load_ff(layout, me_ref, refs, stacked, in_w, down_w, sem):
    if stacked:
        share = layout.sizes["y"] * layout.sizes["c"]
        move_pieces(
            layout, me_ref, ("c", "y", "x", "z"), refs[0],
            [(in_w, refs[0].shape[1], in_w.shape[1] // share, 0)], sem, True,
        )
        move_pieces(
            layout, me_ref, ("c", "x", "y", "z"), refs[1],
            [(down_w, refs[1].shape[1], down_w.shape[1] // share, 0)], sem, True,
        )
    else:
        pltpu.make_async_copy(refs[0], in_w, sem).start()
        pltpu.make_async_copy(refs[1], down_w, sem).start()


def attend_kernel(layout, n_w, me_ref, tok_ref, gb_ref, cols_ref, rows_ref, *rest):
    w_refs = rest[:n_w]
    qkv_ref, att_ref, after_ref, n2_ref, qkv_w, out_w, sems = rest[n_w:]
    load_qo(layout, me_ref, w_refs, qkv_w, out_w, sems.at[0])
    d = tok_ref.shape[1]
    inputs = tok_ref[...].astype(F32)
    xhat, _ = norm_parts(inputs)
    n1 = (xhat * gb_ref[0:1, :] + gb_ref[3:4, :]).astype(BF16)
    wait_all(qkv_w, sems.at[0])
    wait_all(out_w, sems.at[0])
    for j in range(3):
        qkv_ref[:, j * d : (j + 1) * d] = mm(n1, qkv_w[:, j * d : (j + 1) * d]).astype(BF16)
    low_half = lax.broadcasted_iota(jnp.int32, (MAXLEN, LANES), 1) < HEAD_DIM
    for q0, k0, k1 in head_blocks(tok_ref.shape[0]):
        mask = same_sentence(cols_ref, rows_ref, q0, k0, k1)
        for p in range(d // LANES):
            at = lambda j: slice(j * d + p * LANES, j * d + (p + 1) * LANES)
            q2 = two_heads(qkv_ref[q0 : q0 + MAXLEN, at(0)], low_half)
            prob = probabilities(q2, qkv_ref[k0:k1, at(1)], mask).astype(BF16)
            out = mm(prob, qkv_ref[k0:k1, at(2)])
            att_ref[q0 : q0 + MAXLEN, at(0)] = pick_heads(out, low_half).astype(BF16)
    after = inputs + mm(att_ref[...], out_w[...])
    after_ref[...] = after
    xhat, _ = norm_parts(after)
    n2_ref[...] = (xhat * gb_ref[1:2, :] + gb_ref[4:5, :]).astype(BF16)


def attend_back_kernel(layout, n_w, stacked, me_ref, tok_ref, gb_ref, cols_ref, rows_ref, qkv_ref, att_ref, ag_ref, *rest):
    w_refs = rest[:n_w]
    rest = rest[n_w:]
    gtok_ref, gb1_ref = rest[:2]
    g_refs = rest[2 : 2 + n_w]
    qkv_w, out_w, dq_s, dk_s, dv_s, gqkv_s, gout_s, sems = rest[2 + n_w :]
    load_qo(layout, me_ref, w_refs, qkv_w, out_w, sems.at[0])
    d = tok_ref.shape[1]
    scale = 1.0 / math.sqrt(HEAD_DIM)
    after_grad = ag_ref[...]
    attn_grad = after_grad.astype(BF16)
    wait_all(qkv_w, sems.at[0])
    wait_all(out_w, sems.at[0])
    gout_s[...] = mm(att_ref[...], attn_grad, TN).astype(BF16)
    att_grad = mm(attn_grad, out_w[...], NT).astype(BF16)
    dk_s[...] = jnp.zeros_like(dk_s)
    dv_s[...] = jnp.zeros_like(dv_s)
    low_half = lax.broadcasted_iota(jnp.int32, (MAXLEN, LANES), 1) < HEAD_DIM
    for q0, k0, k1 in head_blocks(tok_ref.shape[0]):
        mask = same_sentence(cols_ref, rows_ref, q0, k0, k1)
        for p in range(d // LANES):
            at = lambda j: slice(j * d + p * LANES, j * d + (p + 1) * LANES)
            lanes = at(0)
            q2 = two_heads(qkv_ref[q0 : q0 + MAXLEN, lanes], low_half)
            keys, values = qkv_ref[k0:k1, at(1)], qkv_ref[k0:k1, at(2)]
            prob = probabilities(q2, keys, mask)
            a2 = two_heads(att_grad[q0 : q0 + MAXLEN, lanes], low_half)
            prob_grad = mm(a2, values, NT)
            dv_s[k0:k1, lanes] += mm(prob.astype(BF16), a2, TN)
            inner = jnp.sum(prob_grad * prob, axis=-1, keepdims=True)
            score_grad = (prob * (prob_grad - inner)).astype(BF16)
            dq_s[q0 : q0 + MAXLEN, lanes] = pick_heads(mm(score_grad, keys), low_half)
            dk_s[k0:k1, lanes] += mm(score_grad, q2, TN)
    grads = [
        (dq_s[...] * scale).astype(BF16),
        (dk_s[...] * scale).astype(BF16),
        dv_s[...].astype(BF16),
    ]
    inputs = tok_ref[...].astype(F32)
    xhat, r = norm_parts(inputs)
    n1 = (xhat * gb_ref[0:1, :] + gb_ref[3:4, :]).astype(BF16)
    for j in range(3):
        gqkv_s[:, j * d : (j + 1) * d] = mm(n1, grads[j], TN).astype(BF16)
    if stacked:
        share = layout.sizes["y"] * layout.sizes["c"]
        rows = g_refs[0].shape[1]
        qc, oc = 3 * d // share, d // share
        move_pieces(
            layout, me_ref, ("c", "y", "x", "z"), g_refs[0],
            [(gqkv_s, rows, qc, 0), (gout_s, rows, oc, qc)], sems.at[1], False,
        )
    else:
        pltpu.make_async_copy(gqkv_s, g_refs[0], sems.at[1]).start()
        pltpu.make_async_copy(gout_s, g_refs[1], sems.at[1]).start()
    n1_grad = sum(mm(grads[j], qkv_w[:, j * d : (j + 1) * d], NT) for j in range(3))
    dv, gain, bias = norm_back(xhat, r, gb_ref[0:1, :], n1_grad)
    gtok_ref[...] = after_grad + dv
    gb1_ref[...] = jnp.concatenate([gain, bias], axis=0)
    for ref in g_refs:
        wait_all(ref, sems.at[1])


def feed_kernel(layout, stacked, experts, capacity, me_ref, after_ref, n2_ref, gb_ref, cols_ref, rows_ref, route_ref, cot_ref, in_ref, down_ref, two_ref, gate_ref, send_ref, in_w, down_w, sems):
    load_ff(layout, me_ref, (in_ref, down_ref), stacked, in_w, down_w, sems.at[0])
    ff = in_w.shape[1]
    wait_all(in_w, sems.at[0])
    wait_all(down_w, sems.at[0])
    n2 = n2_ref[...]
    step = 512
    total = after_ref[...]
    for j in range(ff // step):
        hidden = gelu(mm(n2, in_w[:, j * step : (j + 1) * step])).astype(BF16)
        part = mm(hidden, down_w[j * step : (j + 1) * step, :])
        total = part if j == 0 else total + part
    layer_two = after_ref[...] + total
    two_ref[...] = layer_two
    xhat, _ = norm_parts(layer_two)
    n3 = (xhat * gb_ref[2:3, :] + gb_ref[5:6, :]).astype(BF16)
    logits = mm(n3, route_ref[...])
    lane = lax.broadcasted_iota(jnp.int32, logits.shape, 1)
    chosen = [
        jnp.sum(jnp.where(lane == cols_ref[:, c + 1 : c + 2], logits, 0.0), axis=1, keepdims=True)
        for c in range(2)
    ]
    peak = jnp.maximum(chosen[0], chosen[1])
    exps = [jnp.exp(v - peak) for v in chosen]
    gates = [v / (exps[0] + exps[1]) for v in exps]
    gate_ref[...] = jnp.where(lane == 0, gates[0], jnp.where(lane == 1, gates[1], 0.0))
    upstream = cot_ref[...].astype(F32)
    row_grads = [(gates[c] * upstream).astype(BF16) for c in range(2)]
    toks = n2.shape[0]
    chunk = min(512, experts * capacity)
    per = chunk // capacity
    for j in range(experts * capacity // chunk):
        slot = lax.broadcasted_iota(jnp.int32, (chunk, toks), 0) + j * chunk
        hot = [(slot == rows_ref[c + 1 : c + 2, :]).astype(BF16) for c in range(2)]
        rows_in = mm(hot[0] + hot[1], n3).astype(BF16)
        rows_grad = (mm(hot[0], row_grads[0]) + mm(hot[1], row_grads[1])).astype(BF16)
        for e in range(per):
            send_ref[j * per + e, 0] = rows_in[e * capacity : (e + 1) * capacity]
            send_ref[j * per + e, 1] = rows_grad[e * capacity : (e + 1) * capacity]


def feed_back_kernel(layout, stacked, me_ref, after_ref, n2_ref, two_ref, gate_ref, gb_ref, cols_ref, route_ref, cot_ref, ret_ref, in_ref, down_ref, lout_ref, ag_ref, gb23_ref, grout_ref, gin_ref, gdown_ref, in_w, down_w, gin_s, gdown_s, sems):
    load_ff(layout, me_ref, (in_ref, down_ref), stacked, in_w, down_w, sems.at[0])
    toks, d = n2_ref.shape
    ff = in_w.shape[1]
    slots = ret_ref.shape[0] * ret_ref.shape[2]
    slot = lax.broadcasted_iota(jnp.int32, (toks, slots), 1)
    hot = [(slot == cols_ref[:, c + 3 : c + 4]).astype(BF16) for c in range(2)]
    results = ret_ref[:, 0].reshape(slots, d)
    in_grads = ret_ref[:, 1].reshape(slots, d)
    picked = [mm(hot[c], results) for c in range(2)]
    three_grad = mm(hot[0] + hot[1], in_grads)
    gates = [gate_ref[:, c : c + 1] for c in range(2)]
    layer_two = two_ref[...]
    lout_ref[...] = (layer_two + gates[0] * picked[0] + gates[1] * picked[1]).astype(BF16)
    upstream = cot_ref[...].astype(F32)
    gate_grad = [jnp.sum(upstream * v, axis=1, keepdims=True) for v in picked]
    mean = gates[0] * gate_grad[0] + gates[1] * gate_grad[1]
    chosen_grad = [gates[c] * (gate_grad[c] - mean) for c in range(2)]
    lane = lax.broadcasted_iota(jnp.int32, (toks, route_ref.shape[1]), 1)
    logit_grad = sum(
        jnp.where(lane == cols_ref[:, c + 1 : c + 2], chosen_grad[c], 0.0) for c in range(2)
    ).astype(BF16)
    three_grad = three_grad + mm(logit_grad, route_ref[...], NT)
    xhat, r = norm_parts(layer_two)
    n3 = (xhat * gb_ref[2:3, :] + gb_ref[5:6, :]).astype(BF16)
    grout_ref[...] = mm(n3, logit_grad, TN)
    dv, gain3, bias3 = norm_back(xhat, r, gb_ref[2:3, :], three_grad)
    two_grad = upstream + dv
    ffn_grad = two_grad.astype(BF16)
    n2 = n2_ref[...]
    wait_all(in_w, sems.at[0])
    wait_all(down_w, sems.at[0])
    step = 512
    n2_grad = None
    for j in range(ff // step):
        at = slice(j * step, (j + 1) * step)
        hidden, slope = gelu_both(mm(n2, in_w[:, at]))
        gdown_s[at, :] = mm(hidden.astype(BF16), ffn_grad, TN).astype(BF16)
        pre_grad = (mm(ffn_grad, down_w[at, :], NT) * slope).astype(BF16)
        gin_s[:, at] = mm(n2, pre_grad, TN).astype(BF16)
        part = mm(pre_grad, in_w[:, at], NT)
        n2_grad = part if n2_grad is None else n2_grad + part
    if stacked:
        share = layout.sizes["y"] * layout.sizes["c"]
        move_pieces(
            layout, me_ref, ("c", "y", "x", "z"), gin_ref,
            [(gin_s, gin_ref.shape[1], ff // share, 0)], sems.at[1], False,
        )
        move_pieces(
            layout, me_ref, ("c", "x", "y", "z"), gdown_ref,
            [(gdown_s, gdown_ref.shape[1], d // share, 0)], sems.at[1], False,
        )
    else:
        pltpu.make_async_copy(gin_s, gin_ref, sems.at[1]).start()
        pltpu.make_async_copy(gdown_s, gdown_ref, sems.at[1]).start()
    xhat, r = norm_parts(after_ref[...])
    dv, gain2, bias2 = norm_back(xhat, r, gb_ref[1:2, :], n2_grad)
    ag_ref[...] = two_grad + dv
    gb23_ref[...] = jnp.concatenate([gain2, gain3, bias2, bias3], axis=0)
    wait_all(gin_ref, sems.at[1])
    wait_all(gdown_ref, sems.at[1])


def expert_kernel(n_ring, recv_ref, *rest):
    w_refs = rest[:n_ring]
    ret_ref, hid_ref, pg_ref, w_s, acc_s, gacc_s, sems = rest[n_ring:]
    per = w_refs[0].shape[0]
    for s in range(n_ring):
        pltpu.make_async_copy(w_refs[s], w_s.at[pl.ds(s * per, per)], sems.at[s]).start()
    n_src, _, cap, d = recv_ref.shape
    rows = n_src * cap
    f = w_refs[0].shape[2]
    step = min(512, rows)
    acc_s[...] = jnp.zeros_like(acc_s)
    gacc_s[...] = jnp.zeros_like(gacc_s)
    for s in range(n_ring):
        wait_all(w_s.at[pl.ds(s * per, per)], sems.at[s])

    @pl.loop(0, n_ring * per)
    def _(k):
        for j in range(rows // step):
            src = slice(j * step // cap, (j + 1) * step // cap)
            at = slice(j * step, (j + 1) * step)
            x = recv_ref[src, 0].reshape(step, d)
            g = recv_ref[src, 1].reshape(step, d)
            up = w_s[k, 0:d, :]
            hidden, slope = gelu_both(mm(x, up))
            hidden = hidden.astype(BF16)
            hid_ref[k, at, :] = hidden
            hidden_grad = None
            for b in range(d // f):
                down = w_s[k, d + b * f : d + (b + 1) * f, :]
                lanes = slice(b * f, (b + 1) * f)
                acc_s[at, lanes] += mm(hidden, down)
                part = mm(g[:, lanes], down, NT)
                hidden_grad = part if hidden_grad is None else hidden_grad + part
            pre_grad = (hidden_grad * slope).astype(BF16)
            pg_ref[k, at, :] = pre_grad
            gacc_s[at, :] += mm(pre_grad, up, NT)

    for i in range(n_src):
        ret_ref[i, 0] = acc_s[i * cap : (i + 1) * cap, :].astype(BF16)
        ret_ref[i, 1] = gacc_s[i * cap : (i + 1) * cap, :].astype(BF16)


def expert_grad_kernel(recv_ref, hid_ref, pg_ref, out_ref):
    n_src, _, cap, d = recv_ref.shape
    rows = n_src * cap
    f = hid_ref.shape[2]
    x = recv_ref[:, 0].reshape(rows, d)
    g = recv_ref[:, 1].reshape(rows, d)
    out_ref[0, 0:d, :] = mm(x, pg_ref[0], TN).astype(BF16)
    down = mm(hid_ref[0], g, TN).astype(BF16)
    for b in range(d // f):
        out_ref[0, d + b * f : d + (b + 1) * f, :] = down[:, b * f : (b + 1) * f]


def local(sizes, tokens, lengths, task_ids, expert_table, norm_gain, norm_bias, w_qkv, w_out, w_in, w_down, w_router, expert_up, expert_down, cotangent):
    layout = Layout(sizes)
    toks, d = tokens.shape
    local_experts, _, f = expert_up.shape
    assert local_experts == sizes["x"] == 2
    share = sizes["y"] * sizes["c"]
    n_hid = sizes["z"] * sizes["x"]
    experts = share * local_experts
    capacity = 2 * toks // experts
    ff = w_in.shape[1] * share
    stacked = all(w.shape[1] % LANES == 0 for w in (w_qkv, w_out, w_in, w_down))

    def swap(v, axis, by=1):
        return lax.ppermute(v, axis, [(i, i ^ by) for i in range(sizes[axis])])

    def gather_stack(piece, order):
        t = piece[None]
        for axis in order:
            t = jnp.concatenate([t] + [swap(t, axis, by) for by in range(1, sizes[axis])])
        return t

    def reduce_stack(t, order):
        for axis in order:
            n = sizes[axis]
            t = t.reshape((n, t.shape[0] // n) + t.shape[1:])
            total = t[0].astype(F32)
            for by in range(1, n):
                total = total + swap(t[by].astype(BF16), axis, by).astype(F32)
            t = total
        return t[0]

    def gather_whole(w):
        w = lax.all_gather(w.astype(BF16), ("y", "c"), axis=1, tiled=True)
        return lax.all_gather(w, ("z", "x"), axis=0, tiled=True)

    def reduce_whole(g):
        g = lax.psum_scatter(g.astype(F32), ("z", "x"), scatter_dimension=0, tiled=True)
        return lax.psum_scatter(g, ("y", "c"), scatter_dimension=1, tiled=True)

    me = jnp.stack([lax.axis_index(a) for a in AXES]).astype(jnp.int32)
    x_at = lax.axis_index("x")

    small = jnp.concatenate([w_router, norm_gain, norm_bias], axis=1).astype(BF16)
    small = lax.all_gather(small, AXES)
    rc = w_router.shape[1]
    route = small[:, :, :rc].reshape(share, d, rc).transpose(1, 0, 2).reshape(d, experts)
    route = jnp.pad(route, ((0, 0), (0, LANES - experts)))
    gb = small[:n_hid, :, rc:].reshape(d, 6).T.astype(F32)
    gb = jnp.pad(gb, ((0, 2), (0, 0)))

    if stacked:
        qo = (gather_stack(jnp.concatenate([w_qkv, w_out], axis=1).astype(BF16), "zxyc"),)
        ffw = (gather_stack(w_in.astype(BF16), "zxyc"), gather_stack(w_down.astype(BF16), "zyxc"))
    else:
        qo = (gather_whole(w_qkv), gather_whole(w_out))
        ffw = (gather_whole(w_in), gather_whole(w_down))

    def piece_of(at):
        up = lax.dynamic_index_in_dim(expert_up, at, 0, keepdims=False)
        down = lax.dynamic_index_in_dim(expert_down, at, 0, keepdims=False)
        return jnp.concatenate(
            [up] + [down[:, b * f : (b + 1) * f] for b in range(d // f)], axis=0
        ).astype(BF16)

    ring = [(i, (i + 1) % sizes["z"]) for i in range(sizes["z"])]
    blocks = [jnp.stack([piece_of(x_at), swap(piece_of(1 - x_at), "x")])]
    for _ in range(sizes["z"] - 1):
        blocks.append(lax.ppermute(blocks[-1], "z", ring))

    rows, cols = find_routes(lengths, task_ids, expert_table, toks, experts, capacity)

    def sds(shape, dtype):
        return jax.ShapeDtypeStruct(shape, dtype)

    n_w = len(qo)
    w_scratch = [pltpu.VMEM((d, 3 * d), BF16), pltpu.VMEM((d, d), BF16)]
    qkv, attended, after, n2 = pl.pallas_call(
        functools.partial(attend_kernel, layout, n_w),
        out_shape=(sds((toks, 3 * d), BF16), sds((toks, d), BF16), sds((toks, d), F32), sds((toks, d), BF16)),
        in_specs=[smem()] + [vmem()] * 4 + [anywhere()] * n_w,
        out_specs=(vmem(),) * 4,
        scratch_shapes=w_scratch + [pltpu.SemaphoreType.DMA((1,))],
        compiler_params=params(),
        name="attend",
    )(me, tokens, gb, cols, rows, *qo)

    f_scratch = [pltpu.VMEM((d, ff), BF16), pltpu.VMEM((ff, d), BF16)]
    layer_two, gates, send = pl.pallas_call(
        functools.partial(feed_kernel, layout, stacked, experts, capacity),
        out_shape=(sds((toks, d), F32), sds((toks, LANES), F32), sds((experts, 2, capacity, d), BF16)),
        in_specs=[smem()] + [vmem()] * 7 + [anywhere()] * 2,
        out_specs=(vmem(),) * 3,
        scratch_shapes=f_scratch + [pltpu.SemaphoreType.DMA((1,))],
        compiler_params=params(),
        name="feed",
    )(me, after, n2, gb, cols, rows, route, cotangent, *ffw)

    recv = lax.all_to_all(send, ("y", "c", "x"), split_axis=0, concat_axis=0, tiled=True)
    n_ring = sizes["z"]
    pieces = n_ring * 2
    slots = experts * capacity
    ret, hid, pre_grad = pl.pallas_call(
        functools.partial(expert_kernel, n_ring),
        out_shape=(sds(recv.shape, BF16), sds((pieces, slots, f), BF16), sds((pieces, slots, f), BF16)),
        in_specs=[vmem()] + [anywhere()] * n_ring,
        out_specs=(vmem(),) * 3,
        scratch_shapes=[
            pltpu.VMEM((pieces, 2 * d, f), BF16),
            pltpu.VMEM((slots, d), F32),
            pltpu.VMEM((slots, d), F32),
            pltpu.SemaphoreType.DMA((n_ring,)),
        ],
        compiler_params=params(),
        name="experts",
    )(recv, *blocks)
    back = lax.all_to_all(ret, ("y", "c", "x"), split_axis=0, concat_axis=0, tiled=True)

    expert_grads = pl.pallas_call(
        expert_grad_kernel,
        grid=(pieces,),
        out_shape=sds((pieces, 2 * d, f), BF16),
        in_specs=[
            pl.BlockSpec(recv.shape, lambda k: (0, 0, 0, 0)),
            pl.BlockSpec((1, slots, f), lambda k: (k, 0, 0)),
            pl.BlockSpec((1, slots, f), lambda k: (k, 0, 0)),
        ],
        out_specs=pl.BlockSpec((1, 2 * d, f), lambda k: (k, 0, 0)),
        compiler_params=params(),
        name="expert_grads",
    )(recv, hid, pre_grad)
    expert_grads = expert_grads.reshape(n_ring, 2, 2 * d, f)
    moving = None
    for t in range(1, n_ring):
        mine = expert_grads[t]
        moving = mine if moving is None else (moving.astype(F32) + mine.astype(F32)).astype(BF16)
        moving = lax.ppermute(moving, "z", ring)
    summed = expert_grads[0].astype(F32)
    if moving is not None:
        summed = summed + moving.astype(F32)
    other = swap(summed[1].astype(BF16), "x").astype(F32)

    def unpiece(p):
        return p[:d], jnp.concatenate([p[d + b * f : d + (b + 1) * f] for b in range(d // f)], axis=1)

    own_up, own_down = unpiece(summed[0])
    oth_up, oth_down = unpiece(other)
    first = x_at == 0
    grad_up = jnp.where(first, jnp.stack([own_up, oth_up]), jnp.stack([oth_up, own_up]))
    grad_edown = jnp.where(first, jnp.stack([own_down, oth_down]), jnp.stack([oth_down, own_down]))

    if stacked:
        ff_out = (sds(ffw[0].shape, BF16), sds(ffw[1].shape, BF16))
        qo_out = (sds(qo[0].shape, BF16),)
    else:
        ff_out = (sds((d, ff), BF16), sds((ff, d), BF16))
        qo_out = (sds((d, 3 * d), BF16), sds((d, d), BF16))
    layer_out, after_grad, gb23, grad_route, g_in, g_down = pl.pallas_call(
        functools.partial(feed_back_kernel, layout, stacked),
        out_shape=(sds((toks, d), BF16), sds((toks, d), F32), sds((4, d), F32), sds((d, LANES), F32)) + ff_out,
        in_specs=[smem()] + [vmem()] * 9 + [anywhere()] * 2,
        out_specs=(vmem(),) * 4 + (anywhere(),) * 2,
        scratch_shapes=f_scratch + f_scratch + [pltpu.SemaphoreType.DMA((2,))],
        compiler_params=params(),
        name="feed_back",
    )(me, after, n2, layer_two, gates, gb, cols, route, cotangent, back, *ffw)

    out = pl.pallas_call(
        functools.partial(attend_back_kernel, layout, n_w, stacked),
        out_shape=(sds((toks, d), F32), sds((2, d), F32)) + qo_out,
        in_specs=[smem()] + [vmem()] * 7 + [anywhere()] * n_w,
        out_specs=(vmem(),) * 2 + (anywhere(),) * n_w,
        scratch_shapes=w_scratch
        + [pltpu.VMEM((toks, d), F32)] * 3
        + w_scratch
        + [pltpu.SemaphoreType.DMA((2,))],
        compiler_params=params(),
        name="attend_back",
    )(me, tokens, gb, cols, rows, qkv, attended, after_grad, *qo)
    grad_tokens, gb1 = out[:2]

    if stacked:
        grad_in = reduce_stack(g_in, "cyxz")
        grad_down = reduce_stack(g_down, "cxyz")
        g_qo = reduce_stack(out[2], "cyxz")
        qc = w_qkv.shape[1]
        grad_qkv, grad_out = g_qo[:, :qc], g_qo[:, qc:]
    else:
        grad_in, grad_down = reduce_whole(g_in), reduce_whole(g_down)
        grad_qkv, grad_out = reduce_whole(out[2]), reduce_whole(out[3])

    small_grad = jnp.concatenate(
        [gb1[0:1], gb23[0:2], gb1[1:2], gb23[2:4], grad_route[:, :experts].T], axis=0
    )
    small_grad = lax.psum(small_grad, AXES)
    h_at = lax.axis_index("z") * sizes["x"] + x_at
    e_at = lax.axis_index("y") * sizes["c"] + lax.axis_index("c")
    rows_dev = d // n_hid
    mine = lax.dynamic_slice_in_dim(small_grad, h_at * rows_dev, rows_dev, axis=1)
    grad_gain, grad_bias = mine[0:3].T, mine[3:6].T
    grad_router = lax.dynamic_slice_in_dim(mine, 6 + e_at * rc, rc, axis=0).T
    return (
        layer_out,
        grad_tokens,
        grad_gain,
        grad_bias,
        grad_qkv,
        grad_out,
        grad_in,
        grad_down,
        grad_router,
        grad_up,
        grad_edown,
    )


def solution(mesh):
    n_exp, n_hid = mesh.shape["expert"], mesh.shape["hidden"]
    sizes = {"y": n_exp // 2, "c": 2, "z": n_hid // 2, "x": 2}
    fine = Mesh(mesh.devices.reshape(tuple(sizes[a] for a in AXES)), AXES)
    both, exp, hid = AXES, ("y", "c"), ("z", "x")
    return jax.shard_map(
        functools.partial(local, sizes),
        mesh=fine,
        in_specs=(
            P(both, None),
            P(both, None),
            P(both, None),
            P(),
            P(hid, None),
            P(hid, None),
            P(hid, exp),
            P(hid, exp),
            P(hid, exp),
            P(hid, exp),
            P(hid, exp),
            P(exp, None, hid),
            P(exp, hid, None),
            P(both, None),
        ),
        out_specs=(
            P(both, None),
            P(both, None),
            P(hid, None),
            P(hid, None),
            P(hid, exp),
            P(hid, exp),
            P(hid, exp),
            P(hid, exp),
            P(hid, exp),
            P(exp, None, hid),
            P(exp, hid, None),
        ),
        check_vma=False,
    )
```

time: 2430 us -> 433 us (0.18)
  blocking collectives: 1450 us -> 109 us
  waiting for transfers between devices: 779 us -> 106 us
  matrix products: 104 us -> 0 us
  Pallas kernels: 0 us -> 89.8 us
  starting transfers between devices: 9.04 us -> 56.4 us
    unnamed x1 -> x0, blocking collectives: 1280 us -> none
    reduce_scatter x8 -> x0, waiting for transfers between devices: 363 us -> none  [the longest x1 89.8 us: local(): lax.psum_scatter(grad_down, 'hidden', scatter_dimension=0, tiled=True)]
    all_gather x5 -> x0, waiting for transfers between devices: 209 us -> none  [the longest x1 109 us: local(): pieces = lax.all_gather(grad_received, 'hidden', axis=0, tiled=True)]
    unnamed x19 -> x0, waiting for transfers between devices: 181 us -> none
    ppermute x0 -> x44, waiting for transfers between devices: none -> 106 us  [the longest x3 41.2 us: local(): moving = lax.ppermute(moving, 'z', ring)]
    dot_general x26 -> x0, matrix products: 103 us -> none  [the longest x1 13.1 us: local(): jnp.einsum('secd,efd->secf', pieces, down_local, preferred_element_type=j...]
    pallas_call x0 -> x7, Pallas kernels: none -> 89.8 us  [the longest x1 20.3 us: local(): pl.pallas_call(functools.partial(expert_kernel, n_ring), out_shape=(sds(r...]
    all_gather x9 -> x1, blocking collectives: 127 us -> 68.8 us  [local(): small = lax.all_gather(small, AXES)]
  transfers between devices with their start and end apart: 18 -> 46, of which waited for: 16 -> 13; matrix products, arithmetic and copies ran while one was open for 4% -> 13% of each run, Pallas kernels for 0% -> 16%
where the time goes in v1:
time: 433 us; the launch traced here: 427 us
  blocking collectives  109 us (25%)
  waiting for transfers between devices  106 us (24%)
  Pallas kernels  89.8 us (21%)
  starting transfers between devices  56.4 us (13%)
  local copies, waits for them, and re-layouts  42.2 us (10%)
  other arithmetic  21.8 us (5%)
    all_gather x1, blocking collectives, local(): small = lax.all_gather(small, AXES)  68.8 us
    ppermute x38, starting transfers between devices, swap(): return lax.ppermute(v, axis, [(i, i ^ by) for i in range(sizes[axis])])  45.4 us
    ppermute x3, waiting for transfers between devices, local(): moving = lax.ppermute(moving, 'z', ring)  41.2 us
    psum x1, blocking collectives, local(): small_grad = lax.psum(small_grad, AXES)  40.4 us
    ppermute x38, waiting for transfers between devices, swap(): return lax.ppermute(v, axis, [(i, i ^ by) for i in range(sizes[axis])])  37.5 us
    ppermute x3, waiting for transfers between devices, local(): blocks.append(lax.ppermute(blocks[-1], 'z', ring))  27.6 us
    pallas_call x1, Pallas kernels, local(): pl.pallas_call(functools.partial(expert_kernel, n_ring), out_shape=(sds(r...  20.3 us
    pallas_call x1, Pallas kernels, local(): pl.pallas_call(functools.partial(feed_back_kernel, layout, stacked), out_...  18 us
  transfers between devices with their start and end apart: 46, of which 13 were waited for; matrix products, arithmetic and copies ran while one was open for 13% of the time, Pallas kernels for 16%

profile of v1, /device:TPU:0, one launch (start us, length us, event | category | flops | bytes accessed | tf_op | source)
XLA Modules:
  0.0 427.2 jit_solution(6290830374322533903)
XLA Ops:
  2.3 3.0 collective-permute-start.12
  5.3 2.6 collective-permute-start.13
  10.3 3.5 collective-permute-start.7
  19.5 3.8 collective-permute-start.1
  37.2 9.0 %collective-permute-done.3 = bf16[4,64,512]{2,1,0:T(8,128)(2,1)S(1)} collective-permute-done((bf16[4,64,512]{2,1,0:T(8,128)(2,1)S(1)}, bf16[4,64,512]{2,1,0:T(8,128)(2,1)S(1)}, u32[]{:S(2)}, u32[]{:S(2)}) %collective-permute-start.3) | collective-permute-done | bytes 262176 | tf_op jit(solution)/shard_map/ppermute | solution.py:505
  54.9 7.3 %collective-permute-done.4 = bf16[8,64,512]{2,1,0:T(8,128)(2,1)} collective-permute-done((bf16[8,64,512]{2,1,0:T(8,128)(2,1)}, bf16[8,64,512]{2,1,0:T(8,128)(2,1)}, u32[]{:S(2)}, u32[]{:S(2)}) %collective-permute-start.4) | collective-permute-done | bytes 524320 | tf_op jit(solution)/shard_map/ppermute | solution.py:505
  64.2 2.3 constant_dynamic-update-slice_fusion.41
  67.0 2.1 collective-permute-done.10
  69.1 2.1 constant_dynamic-update-slice_fusion.23
  71.3 68.8 %all_gather.4 = bf16[32,64,8]{1,2,0:T(8,128)(2,1)S(1)} all-gather(bf16[1,64,8]{1,2,0:T(8,128)(2,1)S(1)} %pad_maximum_fusion.6), channel_id=1, replica_groups=mesh['y'=2,'c'=2,'z'=4,'x'=2] {'y','c','z','x'}, dimensions={0}, use_global_device_ids=true | all-gather | bytes 33792 | tf_op jit(solution)/shard_map/all_gather | solution.py:535
  143.3 2.5 routes.1
  149.8 9.9 %attend.1 = (bf16[512,1536]{1,0:T(8,128)(2,1)}, bf16[512,512]{1,0:T(8,128)(2,1)}, f32[512,512]{1,0:T(8,128)}, bf16[512,512]{1,0:T(8,128)(2,1)}) custom-call(s32[4]{0:T(128)} %pad_add_fusion.me_ref, bf16[512,512]{1,0:T(8,128)(2,1)} %tok_ref.3, f32[8,512]{1,0:T(8,128)} %pad_convert_fusion.gb_ref, s32[512,8]{1,0:T(8,128)} %get-tuple-element.32.cols_ref, ...), custom_call_target="tpu_custom_call" | custom-call | tf_op jit(solution)/shard_map/attend/pallas_call | solution.py:568
  159.7 2.3 constant_dynamic-update-slice_fusion.47.down_ref
  162.0 2.3 constant_dynamic-update-slice_fusion.29.in_ref
  164.3 10.3 %feed.1 = (f32[512,512]{1,0:T(8,128)}, f32[512,128]{1,0:T(8,128)}, bf16[8,2,128,512]{3,2,1,0:T(8,128)(2,1)}) custom-call(s32[4]{0:T(128)} %pad_add_fusion.me_ref, f32[512,512]{1,0:T(8,128)} %get-tuple-element.34.after_ref, bf16[512,512]{1,0:T(8,128)(2,1)} %get-tuple-element.35.n2_ref, f32[8,512]{1,0:T(8,128)} %pad_convert_fusion.gb_ref, ...), custom_call_target="tpu_custom_call" | custom-call | tf_op jit(solution)/shard_map/feed/pallas_call | solution.py:579
  174.6 3.6 all-to-all-start
  178.6 27.6 %collective-permute-done.21.rest_3_ = bf16[2,1024,256]{2,1,0:T(8,128)(2,1)} collective-permute-done((bf16[2,1024,256]{2,1,0:T(8,128)(2,1)S(1)}, bf16[2,1024,256]{2,1,0:T(8,128)(2,1)}, u32[]{:S(2)}, u32[]{:S(2)}) %collective-permute-start.21) | collective-permute-done | bytes 1048608 | tf_op jit(solution)/shard_map/ppermute | solution.py:559
  207.5 20.3 %experts.1 = (bf16[8,2,128,512]{3,2,1,0:T(8,128)(2,1)}, bf16[8,1024,256]{2,1,0:T(8,128)(2,1)}, bf16[8,1024,256]{2,1,0:T(8,128)(2,1)}) custom-call(bf16[8,2,128,512]{3,2,1,0:T(8,128)(2,1)} %copy-done, bf16[2,1024,256]{2,1,0:T(8,128)(2,1)} %copy-done.3, bf16[2,1024,256]{2,1,0:T(8,128)(2,1)} %collective-permute-done.19.rest_1_, ...), custom_call_target="tpu_custom_call" | custom-call | tf_op jit(solution)/shard_map/experts/pallas_call | solution.py:593
  227.8 3.9 all-to-all-start.1
  231.7 11.0 %expert_grads.1 = bf16[8,1024,256]{2,1,0:T(8,128)(2,1)} custom-call(bf16[8,2,128,512]{3,2,1,0:T(8,128)(2,1)} %copy-done, bf16[8,1024,256]{2,1,0:T(8,128)(2,1)} %get-tuple-element.51.hid_ref, bf16[8,1024,256]{2,1,0:T(8,128)(2,1)} %get-tuple-element.52.pg_ref), custom_call_target="tpu_custom_call" | custom-call | tf_op jit(solution)/shard_map/expert_grads/pallas_call | solution.py:609
  244.1 27.4 %collective-permute-done.40 = bf16[2,1024,256]{2,1,0:T(8,128)(2,1)S(1)} collective-permute-done((bf16[2,1024,256]{2,1,0:T(8,128)(2,1)S(1)}, bf16[2,1024,256]{2,1,0:T(8,128)(2,1)S(1)}, u32[]{:S(2)}, u32[]{:S(2)}) %collective-permute-start.40) | collective-permute-done | bytes 1048608 | tf_op jit(solution)/shard_map/ppermute | solution.py:627
  274.4 18.0 %feed_back.1 = (bf16[512,512]{1,0:T(8,128)(2,1)}, f32[512,512]{1,0:T(8,128)}, f32[4,512]{1,0:T(4,128)}, f32[512,128]{1,0:T(8,128)}, bf16[32,64,512]{2,1,0:T(8,128)(2,1)}, /*index=5*/bf16[32,256,128]{2,1,0:T(8,128)(2,1)}) custom-call(s32[4]{0:T(128)} %pad_add_fusion.me_ref, f32[512,512]{1,0:T(8,128)} %get-tuple-element.34.after_ref, ...), custom_call_target="tpu_custom_call" | custom-call | tf_op jit(solution)/shard_map/feed_back/pallas_call | solution.py:648
  292.5 2.5 slice.269
  296.5 17.7 %attend_back.1 = (f32[512,512]{1,0:T(8,128)}, f32[2,512]{1,0:T(2,128)}, bf16[32,64,512]{2,1,0:T(8,128)(2,1)}) custom-call(s32[4]{0:T(128)} %pad_add_fusion.me_ref, bf16[512,512]{1,0:T(8,128)(2,1)} %tok_ref.3, f32[8,512]{1,0:T(8,128)} %pad_convert_fusion.gb_ref, s32[512,8]{1,0:T(8,128)} %get-tuple-element.32.cols_ref, s32[8,512]{1,0:T(8,128)} %get-tuple-element.33.rows_ref, ...), custom_call_target="tpu_custom_call" | custom-call | tf_op jit(solution)/shard_map/attend_back/pallas_call | solution.py:658
  314.2 2.3 slice.247
  316.8 40.4 %psum.7 = f32[14,512]{1,0:T(8,128)S(1)} all-reduce(f32[14,512]{1,0:T(8,128)S(1)} %concatenate.128), channel_id=1, replica_groups=mesh['y'=2,'c'=2,'z'=4,'x'=2] {'y','c','z','x'}, use_global_device_ids=true, to_apply=%region_0.1 | all-reduce | flops 7168 | bytes 57344 | tf_op jit(solution)/shard_map/psum | solution.py:685
  359.7 2.4 collective-permute-start.42
  364.3 2.3 collective-permute-start.35
  372.0 13.9 %collective-permute-done.42 = bf16[2,1024,256]{2,1,0:T(8,128)(2,1)S(1)} collective-permute-done((bf16[2,1024,256]{2,1,0:T(8,128)(2,1)S(1)}, bf16[2,1024,256]{2,1,0:T(8,128)(2,1)S(1)}, u32[]{:S(2)}, u32[]{:S(2)}) %collective-permute-start.42) | collective-permute-done | bytes 1048608 | tf_op jit(solution)/shard_map/ppermute | solution.py:627
  393.4 3.1 collective-permute-done.36
  399.0 9.0 %collective-permute-done.30 = bf16[4,64,512]{2,1,0:T(8,128)(2,1)S(1)} collective-permute-done((bf16[4,64,512]{2,1,0:T(8,128)(2,1)S(1)}, bf16[4,64,512]{2,1,0:T(8,128)(2,1)S(1)}, u32[]{:S(2)}, u32[]{:S(2)}) %collective-permute-start.30) | collective-permute-done | bytes 262176 | tf_op jit(solution)/shard_map/ppermute | solution.py:505
  416.7 2.9 collective-permute-start.27
  (204 shorter events, 85.5 us)
Async XLA Ops:
  2.3 16.6 %collective-permute-start.12 = (bf16[1,256,128]{2,1,0:T(8,128)(2,1)S(1)}, bf16[1,256,128]{2,1,0:T(8,128)(2,1)S(1)}, u32[]{:S(2)}, u32[]{:S(2)}) collective-permute-start(bf16[1,256,128]{2,1,0:T(8,128)(2,1)S(1)} %get-tuple-element.82), channel_id=1, source_target_pairs={{0,2},{2,0},{4,6},{6,4},{1,3},{3,1},{5,7},{7,5},{8,10},{10,8},{12,... | collective-permute-start | bytes 196616 | tf_op jit(solution)/shard_map/ppermute | solution.py:505
  9.5 13.9 %collective-permute-start.6 = (bf16[1,64,512]{2,1,0:T(8,128)(2,1)S(1)}, bf16[1,64,512]{2,1,0:T(8,128)(2,1)S(1)}, u32[]{:S(2)}, u32[]{:S(2)}) collective-permute-start(bf16[1,64,512]{2,1,0:T(8,128)(2,1)S(1)} %get-tuple-element.84), channel_id=1, source_target_pairs={{0,2},{2,0},{4,6},{6,4},{1,3},{3,1},{5,7},{7,5},{8,10},{10,8},{12,... | collective-permute-start | bytes 196616 | tf_op jit(solution)/shard_map/ppermute | solution.py:505
  23.5 29.7 %collective-permute-start.18 = (bf16[1024,256]{1,0:T(8,128)(2,1)S(1)}, bf16[1024,256]{1,0:T(8,128)(2,1)}, u32[]{:S(2)}, u32[]{:S(2)}) collective-permute-start(bf16[1024,256]{1,0:T(8,128)(2,1)S(1)} %pad_maximum_fusion.1), channel_id=1, source_target_pairs={{0,1},{1,0},{2,3},{3,2},{4,5},{5,4},{6,7},{7,6},{8,9},{9,8},{10,11... | collective-permute-start | bytes 1572872 | tf_op jit(solution)/shard_map/ppermute | solution.py:505
  25.2 23.4 %collective-permute-start.15 = (bf16[4,256,128]{2,1,0:T(8,128)(2,1)S(1)}, bf16[4,256,128]{2,1,0:T(8,128)(2,1)S(1)}, u32[]{:S(2)}, u32[]{:S(2)}) collective-permute-start(bf16[4,256,128]{2,1,0:T(8,128)(2,1)S(1)} %pad_maximum_fusion.4), channel_id=1, source_target_pairs={{0,16},{16,0},{1,17},{17,1},{2,18},{18,2},{3,19},{19,3},{4,20},{20... | collective-permute-start | bytes 786440 | tf_op jit(solution)/shard_map/ppermute | solution.py:505
  26.7 24.3 %collective-permute-start.9 = (bf16[4,64,512]{2,1,0:T(8,128)(2,1)S(1)}, bf16[4,64,512]{2,1,0:T(8,128)(2,1)S(1)}, u32[]{:S(2)}, u32[]{:S(2)}) collective-permute-start(bf16[4,64,512]{2,1,0:T(8,128)(2,1)S(1)} %pad_maximum_fusion.3), channel_id=1, source_target_pairs={{0,1},{1,0},{2,3},{3,2},{4,5},{5,4},{6,7},{7,6},{8,9},{9,8},{10,11... | collective-permute-start | bytes 786440 | tf_op jit(solution)/shard_map/ppermute | solution.py:505
  29.5 16.7 %collective-permute-start.3 = (bf16[4,64,512]{2,1,0:T(8,128)(2,1)S(1)}, bf16[4,64,512]{2,1,0:T(8,128)(2,1)S(1)}, u32[]{:S(2)}, u32[]{:S(2)}) collective-permute-start(bf16[4,64,512]{2,1,0:T(8,128)(2,1)S(1)} %pad_maximum_fusion.2), channel_id=1, source_target_pairs={{0,1},{1,0},{2,3},{3,2},{4,5},{5,4},{6,7},{7,6},{8,9},{9,8},{10,11... | collective-permute-start | bytes 786440 | tf_op jit(solution)/shard_map/ppermute | solution.py:505
  47.0 15.2 %collective-permute-start.4 = (bf16[8,64,512]{2,1,0:T(8,128)(2,1)}, bf16[8,64,512]{2,1,0:T(8,128)(2,1)}, u32[]{:S(2)}, u32[]{:S(2)}) collective-permute-start(bf16[8,64,512]{2,1,0:T(8,128)(2,1)} %get-tuple-element.120), channel_id=1, source_target_pairs={{0,16},{16,0},{1,17},{17,1},{2,18},{18,2},{3,19},{19,3},{4,20},{20... | collective-permute-start | bytes 1572872 | tf_op jit(solution)/shard_map/ppermute | solution.py:505
  49.6 14.7 %collective-permute-start.16 = (bf16[8,256,128]{2,1,0:T(8,128)(2,1)}, bf16[8,256,128]{2,1,0:T(8,128)(2,1)}, u32[]{:S(2)}, u32[]{:S(2)}) collective-permute-start(bf16[8,256,128]{2,1,0:T(8,128)(2,1)} %get-tuple-element.114), channel_id=1, source_target_pairs={{0,1},{1,0},{2,3},{3,2},{4,5},{5,4},{6,7},{7,6},{8,9},{9,8},{10,11... | collective-permute-start | bytes 1572872 | tf_op jit(solution)/shard_map/ppermute | solution.py:505
  52.0 17.1 %collective-permute-start.10 = (bf16[8,64,512]{2,1,0:T(8,128)(2,1)}, bf16[8,64,512]{2,1,0:T(8,128)(2,1)}, u32[]{:S(2)}, u32[]{:S(2)}) collective-permute-start(bf16[8,64,512]{2,1,0:T(8,128)(2,1)} %get-tuple-element.117), channel_id=1, source_target_pairs={{0,16},{16,0},{1,17},{17,1},{2,18},{18,2},{3,19},{19,3},{4,20},{20... | collective-permute-start | bytes 1572872 | tf_op jit(solution)/shard_map/ppermute | solution.py:505
  54.3 92.7 %collective-permute-start.19 = (bf16[2,1024,256]{2,1,0:T(8,128)(2,1)S(1)}, bf16[2,1024,256]{2,1,0:T(8,128)(2,1)}, u32[]{:S(2)}, u32[]{:S(2)}) collective-permute-start(bf16[2,1024,256]{2,1,0:T(8,128)(2,1)S(1)} %pad_maximum_fusion.rest_0_), channel_id=1, source_target_pairs={{0,2},{2,4},{4,6},{6,0},{1,3},{3,5},{5,7},{7,1},{8,10},{10,12},{12... | collective-permute-start | bytes 3145736 | tf_op jit(solution)/shard_map/ppermute | solution.py:559
  64.2 82.9 %collective-permute-start.5 = (bf16[16,64,512]{2,1,0:T(8,128)(2,1)}, bf16[16,64,512]{2,1,0:T(8,128)(2,1)}, u32[]{:S(2)}, u32[]{:S(2)}) collective-permute-start(bf16[16,64,512]{2,1,0:T(8,128)(2,1)} %get-tuple-element.97), channel_id=1, source_target_pairs={{0,8},{8,0},{1,9},{9,1},{2,10},{10,2},{3,11},{11,3},{4,12},{12,4},... | collective-permute-start | bytes 3145736 | tf_op jit(solution)/shard_map/ppermute | solution.py:505
  66.5 93.2 %collective-permute-start.17 = (bf16[16,256,128]{2,1,0:T(8,128)(2,1)}, bf16[16,256,128]{2,1,0:T(8,128)(2,1)}, u32[]{:S(2)}, u32[]{:S(2)}) collective-permute-start(bf16[16,256,128]{2,1,0:T(8,128)(2,1)} %get-tuple-element.93), channel_id=1, source_target_pairs={{0,8},{8,0},{1,9},{9,1},{2,10},{10,2},{3,11},{11,3},{4,12},{12,4},... | collective-permute-start | bytes 3145736 | tf_op jit(solution)/shard_map/ppermute | solution.py:505
  71.2 90.8 %collective-permute-start.11 = (bf16[16,64,512]{2,1,0:T(8,128)(2,1)}, bf16[16,64,512]{2,1,0:T(8,128)(2,1)}, u32[]{:S(2)}, u32[]{:S(2)}) collective-permute-start(bf16[16,64,512]{2,1,0:T(8,128)(2,1)} %get-tuple-element.95), channel_id=1, source_target_pairs={{0,8},{8,0},{1,9},{9,1},{2,10},{10,2},{3,11},{11,3},{4,12},{12,4},... | collective-permute-start | bytes 3145736 | tf_op jit(solution)/shard_map/ppermute | solution.py:505
  147.0 31.3 %collective-permute-start.20 = (bf16[2,1024,256]{2,1,0:T(8,128)(2,1)}, bf16[2,1024,256]{2,1,0:T(8,128)(2,1)S(1)}, u32[]{:S(2)}, u32[]{:S(2)}) collective-permute-start(bf16[2,1024,256]{2,1,0:T(8,128)(2,1)} %collective-permute-done.19.rest_1_), channel_id=1, source_target_pairs={{0,2},{2,4},{4,6},{6,0},{1,3},{3,5},{5,7},{7,1},{8,10},{10,12},{12... | collective-permute-start | bytes 3145736 | tf_op jit(solution)/shard_map/ppermute | solution.py:559
  174.6 31.5 %all-to-all-start = ((bf16[8,2,128,512]{3,2,1,0:T(8,128)(2,1)}), bf16[8,2,128,512]{3,2,1,0:T(8,128)(2,1)S(1)}, u32[]{:S(2)}, u32[]{:S(2)}) async-start(bf16[8,2,128,512]{3,2,1,0:T(8,128)(2,1)} %get-tuple-element.38), calls=%async_computation | async-start | bytes 4194304 | tf_op jit(solution)/shard_map/all_to_all | solution.py:589
  178.3 27.9 %collective-permute-start.21 = (bf16[2,1024,256]{2,1,0:T(8,128)(2,1)S(1)}, bf16[2,1024,256]{2,1,0:T(8,128)(2,1)}, u32[]{:S(2)}, u32[]{:S(2)}) collective-permute-start(bf16[2,1024,256]{2,1,0:T(8,128)(2,1)S(1)} %collective-permute-done.20.rest_2_), channel_id=1, source_target_pairs={{0,2},{2,4},{4,6},{6,0},{1,3},{3,5},{5,7},{7,1},{8,10},{10,12},{12... | collective-permute-start | bytes 3145736 | tf_op jit(solution)/shard_map/ppermute | solution.py:559
  227.8 45.2 %all-to-all-start.1 = ((bf16[8,2,128,512]{3,2,1,0:T(8,128)(2,1)}), bf16[8,2,128,512]{3,2,1,0:T(8,128)(2,1)S(1)}, u32[]{:S(2)}, u32[]{:S(2)}) async-start(bf16[8,2,128,512]{3,2,1,0:T(8,128)(2,1)} %get-tuple-element.39), calls=%async_computation.1 | async-start | bytes 4194304 | tf_op jit(solution)/shard_map/all_to_all | solution.py:607
  244.0 27.4 %collective-permute-start.40 = (bf16[2,1024,256]{2,1,0:T(8,128)(2,1)S(1)}, bf16[2,1024,256]{2,1,0:T(8,128)(2,1)S(1)}, u32[]{:S(2)}, u32[]{:S(2)}) collective-permute-start(bf16[2,1024,256]{2,1,0:T(8,128)(2,1)S(1)} %slice.324), channel_id=1, source_target_pairs={{0,2},{2,4},{4,6},{6,0},{1,3},{3,5},{5,7},{7,1},{8,10},{10,12},{12... | collective-permute-start | bytes 3145736 | tf_op jit(solution)/shard_map/ppermute | solution.py:627
  273.0 84.9 %collective-permute-start.41 = (bf16[2,1024,256]{2,1,0:T(8,128)(2,1)S(1)}, bf16[2,1024,256]{2,1,0:T(8,128)(2,1)}, u32[]{:S(2)}, u32[]{:S(2)}) collective-permute-start(bf16[2,1024,256]{2,1,0:T(8,128)(2,1)S(1)} %add_convert_fusion.1), channel_id=1, source_target_pairs={{0,2},{2,4},{4,6},{6,0},{1,3},{3,5},{5,7},{7,1},{8,10},{10,12},{12... | collective-permute-start | bytes 3145736 | tf_op jit(solution)/shard_map/ppermute | solution.py:627
  294.9 67.8 %collective-permute-start.34 = (bf16[16,256,128]{2,1,0:T(8,128)(2,1)}, bf16[16,256,128]{2,1,0:T(8,128)(2,1)}, u32[]{:S(2)}, u32[]{:S(2)}) collective-permute-start(bf16[16,256,128]{2,1,0:T(8,128)(2,1)} %slice.269), channel_id=1, source_target_pairs={{0,8},{8,0},{1,9},{9,1},{2,10},{10,2},{3,11},{11,3},{4,12},{12,4},... | collective-permute-start | bytes 3145736 | tf_op jit(solution)/shard_map/ppermute | solution.py:505
  296.0 70.6 %collective-permute-start.28 = (bf16[16,64,512]{2,1,0:T(8,128)(2,1)}, bf16[16,64,512]{2,1,0:T(8,128)(2,1)}, u32[]{:S(2)}, u32[]{:S(2)}) collective-permute-start(bf16[16,64,512]{2,1,0:T(8,128)(2,1)} %slice.259), channel_id=1, source_target_pairs={{0,8},{8,0},{1,9},{9,1},{2,10},{10,2},{3,11},{11,3},{4,12},{12,4},... | collective-permute-start | bytes 3145736 | tf_op jit(solution)/shard_map/ppermute | solution.py:505
  316.5 52.4 %collective-permute-start.22 = (bf16[16,64,512]{2,1,0:T(8,128)(2,1)}, bf16[16,64,512]{2,1,0:T(8,128)(2,1)}, u32[]{:S(2)}, u32[]{:S(2)}) collective-permute-start(bf16[16,64,512]{2,1,0:T(8,128)(2,1)} %slice.247), channel_id=1, source_target_pairs={{0,8},{8,0},{1,9},{9,1},{2,10},{10,2},{3,11},{11,3},{4,12},{12,4},... | collective-permute-start | bytes 3145736 | tf_op jit(solution)/shard_map/ppermute | solution.py:505
  359.7 26.2 %collective-permute-start.42 = (bf16[2,1024,256]{2,1,0:T(8,128)(2,1)S(1)}, bf16[2,1024,256]{2,1,0:T(8,128)(2,1)S(1)}, u32[]{:S(2)}, u32[]{:S(2)}) collective-permute-start(bf16[2,1024,256]{2,1,0:T(8,128)(2,1)S(1)} %add_convert_fusion), channel_id=1, source_target_pairs={{0,2},{2,4},{4,6},{6,0},{1,3},{3,5},{5,7},{7,1},{8,10},{10,12},{12... | collective-permute-start | bytes 3145736 | tf_op jit(solution)/shard_map/ppermute | solution.py:627
  364.3 24.7 %collective-permute-start.35 = (bf16[8,256,128]{2,1,0:T(8,128)(2,1)S(1)}, bf16[8,256,128]{2,1,0:T(8,128)(2,1)S(1)}, u32[]{:S(2)}, u32[]{:S(2)}) collective-permute-start(bf16[8,256,128]{2,1,0:T(8,128)(2,1)S(1)} %slice.382), channel_id=1, source_target_pairs={{0,1},{1,0},{2,3},{3,2},{4,5},{5,4},{6,7},{7,6},{8,9},{9,8},{10,11... | collective-permute-start | bytes 1572872 | tf_op jit(solution)/shard_map/ppermute | solution.py:505
  368.2 22.5 %collective-permute-start.29 = (bf16[8,64,512]{2,1,0:T(8,128)(2,1)S(1)}, bf16[8,64,512]{2,1,0:T(8,128)(2,1)S(1)}, u32[]{:S(2)}, u32[]{:S(2)}) collective-permute-start(bf16[8,64,512]{2,1,0:T(8,128)(2,1)S(1)} %slice.383), channel_id=1, source_target_pairs={{0,16},{16,0},{1,17},{17,1},{2,18},{18,2},{3,19},{19,3},{4,20},{20... | collective-permute-start | bytes 1572872 | tf_op jit(solution)/shard_map/ppermute | solution.py:505
  370.5 21.9 %collective-permute-start.23 = (bf16[8,64,512]{2,1,0:T(8,128)(2,1)S(1)}, bf16[8,64,512]{2,1,0:T(8,128)(2,1)S(1)}, u32[]{:S(2)}, u32[]{:S(2)}) collective-permute-start(bf16[8,64,512]{2,1,0:T(8,128)(2,1)S(1)} %slice.384), channel_id=1, source_target_pairs={{0,16},{16,0},{1,17},{17,1},{2,18},{18,2},{3,19},{19,3},{4,20},{20... | collective-permute-start | bytes 1572872 | tf_op jit(solution)/shard_map/ppermute | solution.py:505
  387.5 21.5 %collective-permute-start.43 = (bf16[1024,256]{1,0:T(8,128)(2,1)S(1)}, bf16[1024,256]{1,0:T(8,128)(2,1)S(1)}, u32[]{:S(2)}, u32[]{:S(2)}) collective-permute-start(bf16[1024,256]{1,0:T(8,128)(2,1)S(1)} %fusion), channel_id=1, source_target_pairs={{0,1},{1,0},{2,3},{3,2},{4,5},{5,4},{6,7},{7,6},{8,9},{9,8},{10,11... | collective-permute-start | bytes 1572872 | tf_op jit(solution)/shard_map/ppermute | solution.py:505
  390.9 17.1 %collective-permute-start.30 = (bf16[4,64,512]{2,1,0:T(8,128)(2,1)S(1)}, bf16[4,64,512]{2,1,0:T(8,128)(2,1)S(1)}, u32[]{:S(2)}, u32[]{:S(2)}) collective-permute-start(bf16[4,64,512]{2,1,0:T(8,128)(2,1)S(1)} %slice.386), channel_id=1, source_target_pairs={{0,1},{1,0},{2,3},{3,2},{4,5},{5,4},{6,7},{7,6},{8,9},{9,8},{10,11... | collective-permute-start | bytes 786440 | tf_op jit(solution)/shard_map/ppermute | solution.py:505
  392.6 18.2 %collective-permute-start.24 = (bf16[4,64,512]{2,1,0:T(8,128)(2,1)S(1)}, bf16[4,64,512]{2,1,0:T(8,128)(2,1)S(1)}, u32[]{:S(2)}, u32[]{:S(2)}) collective-permute-start(bf16[4,64,512]{2,1,0:T(8,128)(2,1)S(1)} %slice.387), channel_id=1, source_target_pairs={{0,1},{1,0},{2,3},{3,2},{4,5},{5,4},{6,7},{7,6},{8,9},{9,8},{10,11... | collective-permute-start | bytes 786440 | tf_op jit(solution)/shard_map/ppermute | solution.py:505
  396.7 18.5 %collective-permute-start.37 = (bf16[1,256,128]{2,1,0:T(8,128)(2,1)S(1)}, bf16[1,256,128]{2,1,0:T(8,128)(2,1)S(1)}, u32[]{:S(2)}, u32[]{:S(2)}) collective-permute-start(bf16[1,256,128]{2,1,0:T(8,128)(2,1)S(1)} %get-tuple-element.99), channel_id=1, source_target_pairs={{0,2},{2,0},{4,6},{6,4},{1,3},{3,1},{5,7},{7,5},{8,10},{10,8},{12,... | collective-permute-start | bytes 196616 | tf_op jit(solution)/shard_map/ppermute | solution.py:505
  398.1 17.1 %collective-permute-start.38 = (bf16[1,256,128]{2,1,0:T(8,128)(2,1)S(1)}, bf16[1,256,128]{2,1,0:T(8,128)(2,1)S(1)}, u32[]{:S(2)}, u32[]{:S(2)}) collective-permute-start(bf16[1,256,128]{2,1,0:T(8,128)(2,1)S(1)} %get-tuple-element.101), channel_id=1, source_target_pairs={{0,4},{2,6},{4,0},{6,2},{1,5},{3,7},{5,1},{7,3},{8,12},{10,14},{12... | collective-permute-start | bytes 196616 | tf_op jit(solution)/shard_map/ppermute | solution.py:505
  409.1 15.2 %collective-permute-start.31 = (bf16[1,64,512]{2,1,0:T(8,128)(2,1)S(1)}, bf16[1,64,512]{2,1,0:T(8,128)(2,1)S(1)}, u32[]{:S(2)}, u32[]{:S(2)}) collective-permute-start(bf16[1,64,512]{2,1,0:T(8,128)(2,1)S(1)} %get-tuple-element.102), channel_id=1, source_target_pairs={{0,2},{2,0},{4,6},{6,4},{1,3},{3,1},{5,7},{7,5},{8,10},{10,8},{12,... | collective-permute-start | bytes 196616 | tf_op jit(solution)/shard_map/ppermute | solution.py:505
  (32 other events, 468.6 us)
